TPU v7x, 512 devices: a whole 4x4x16 slice. The times are simulated.
512 devices in a mesh: lat: 8 (over y, x_hi), lon: 64 (over z, x_lo, core).
Axes of the slice: x: 4 (x_hi: 2, x_lo: 2; x = x_hi * 2 + x_lo), y: 4, z: 16, core: 2. Of those that a mesh axis runs over, the one named last changes fastest.
Arguments:
- tokens: bfloat16 [96, 768, 512], P('lat', 'lon'), may hold values from -40 to 40
- cotangent: bfloat16 [96, 768, 512], P('lat', 'lon'), may hold values from -48 to 48
- w_query: bfloat16 [512, 512], replicated, may hold values from -0.25 to 0.25
- w_key: bfloat16 [512, 512], replicated, may hold values from -0.25 to 0.25
- w_value: bfloat16 [512, 512], replicated, may hold values from -0.25 to 0.25
- w_output: bfloat16 [512, 512], replicated, may hold values from -0.25 to 0.25
Outputs:
- d_tokens: bfloat16 [96, 768, 512], P('lat', 'lon')
- d_output: float32 [512, 512], replicated
All inputs are finite; a program needn't handle non-finite values.
Results may differ from a plain program's by a relative error of at most 0.01.
The roundings to bfloat16 on the way count: a program that leaves them out, or rounds other values in their place, can miss the bound.
Values may be sent and summed in bfloat16 or wider, within the bound.
No kernel may reach another device: no remote copies, remote signals or barrier semaphores. Data moves between devices by JAX's collectives and lax.ppermute only.
A program may use at most 64 MiB of HBM per device.

v0:
```python
import math

import jax
import jax.numpy as jnp
from jax import lax
from jax.sharding import PartitionSpec as P

HEADS = 16
WIN = 12
SHIFT = 6


def from_behind(value, axis, steps):
    count = lax.axis_size(axis)
    pairs = [(source, (source + steps) % count) for source in range(count)]
    return lax.ppermute(value, axis, pairs)


def to_windows(field, window):
    n_rows, n_cols, depth = field.shape
    blocks = field.reshape(n_rows // window, window, n_cols // window, window, depth)
    return blocks.transpose(0, 2, 1, 3, 4).reshape(-1, window * window, depth)


def from_windows(packed, window, n_rows, n_cols):
    depth = packed.shape[-1]
    blocks = packed.reshape(n_rows // window, n_cols // window, window, window, depth)
    return blocks.transpose(0, 2, 1, 3, 4).reshape(n_rows, n_cols, depth)


def window_backward(windows, cot_windows, labels, w_query, w_key, w_value, w_output, n_heads):
    n_win, n_pts, model_width = windows.shape
    head_dim = model_width // n_heads
    factor_qk = 1.0 / math.sqrt(head_dim)
    flat_tokens = windows.reshape(n_win * n_pts, model_width)
    w_joint = jnp.concatenate([w_query, w_key, w_value], axis=1)
    projected = jnp.dot(flat_tokens, w_joint, preferred_element_type=jnp.float32).astype(
        jnp.bfloat16
    )
    shaped = projected.reshape(n_win, n_pts, 3, n_heads, head_dim)
    queries = shaped[:, :, 0]
    key_rows = shaped[:, :, 1]
    value_rows = shaped[:, :, 2]
    logits = factor_qk * jnp.einsum(
        "wqhd,wkhd->whqk", queries, key_rows, preferred_element_type=jnp.float32
    )
    allowed = (labels[:, :, None] == labels[:, None, :])[:, None]
    logits = jnp.where(allowed, logits, -1e30)
    peak = jnp.max(logits, axis=-1, keepdims=True)
    raised = jnp.exp(logits - peak)
    probs = raised / jnp.sum(raised, axis=-1, keepdims=True)
    probs_low = probs.astype(jnp.bfloat16)
    attended = jnp.einsum(
        "whqk,wkhd->wqhd", probs_low, value_rows, preferred_element_type=jnp.float32
    ).astype(jnp.bfloat16)
    attended_flat = attended.reshape(n_win * n_pts, model_width)
    upstream = cot_windows.reshape(n_win * n_pts, model_width)
    output_term = lax.dot_general(
        attended_flat, upstream, (((0,), (0,)), ((), ())), preferred_element_type=jnp.float32
    )
    d_attended = lax.dot_general(
        upstream, w_output, (((1,), (1,)), ((), ())), preferred_element_type=jnp.float32
    )
    d_attended = d_attended.astype(jnp.bfloat16).reshape(n_win, n_pts, n_heads, head_dim)
    d_probs = jnp.einsum(
        "wqhd,wkhd->whqk", d_attended, value_rows, preferred_element_type=jnp.float32
    )
    d_values = jnp.einsum(
        "whqk,wqhd->wkhd", probs_low, d_attended, preferred_element_type=jnp.float32
    ).astype(jnp.bfloat16)
    row_inner = jnp.sum(probs * d_probs, axis=-1, keepdims=True)
    d_logits = (factor_qk * probs * (d_probs - row_inner)).astype(jnp.bfloat16)
    d_queries = jnp.einsum(
        "whqk,wkhd->wqhd", d_logits, key_rows, preferred_element_type=jnp.float32
    ).astype(jnp.bfloat16)
    d_keys = jnp.einsum(
        "whqk,wqhd->wkhd", d_logits, queries, preferred_element_type=jnp.float32
    ).astype(jnp.bfloat16)
    joined = jnp.stack([d_queries, d_keys, d_values], axis=2).reshape(
        n_win * n_pts, 3 * model_width
    )
    d_flat = lax.dot_general(
        joined, w_joint, (((1,), (1,)), ((), ())), preferred_element_type=jnp.float32
    )
    return (d_flat.reshape(n_win, n_pts, model_width), output_term)


def per_device(tokens, cotangent, w_query, w_key, w_value, w_output):
    n_rows, n_cols, model_width = tokens.shape
    below = from_behind((tokens[:SHIFT], cotangent[:SHIFT]), "lat", -1)
    lat_tokens = jnp.concatenate([tokens[SHIFT:], below[0]], axis=0)
    lat_cot = jnp.concatenate([cotangent[SHIFT:], below[1]], axis=0)
    beside = from_behind((lat_tokens[:, :SHIFT], lat_cot[:, :SHIFT]), "lon", -1)
    tile_tokens = jnp.concatenate([lat_tokens[:, SHIFT:], beside[0]], axis=1)
    tile_cot = jnp.concatenate([lat_cot[:, SHIFT:], beside[1]], axis=1)
    total_rows = n_rows * lax.axis_size("lat")
    global_rows = lax.axis_index("lat") * n_rows + jnp.arange(n_rows, dtype=jnp.int32)
    region = (global_rows >= total_rows - SHIFT).astype(jnp.int32)
    labels_tile = jnp.broadcast_to(region[:, None, None], (n_rows, n_cols, 1))
    labels = to_windows(labels_tile, WIN)[:, :, 0]
    d_win, output_term = window_backward(
        to_windows(tile_tokens, WIN),
        to_windows(tile_cot, WIN),
        labels,
        w_query,
        w_key,
        w_value,
        w_output,
        HEADS,
    )
    d_tile = from_windows(d_win.astype(jnp.bfloat16), WIN, n_rows, n_cols)
    from_left = from_behind(d_tile[:, n_cols - SHIFT :], "lon", 1)
    lon_back = jnp.concatenate([from_left, d_tile[:, : n_cols - SHIFT]], axis=1)
    from_above = from_behind(lon_back[n_rows - SHIFT :], "lat", 1)
    d_tokens = jnp.concatenate([from_above, lon_back[: n_rows - SHIFT]], axis=0)
    summed = lax.psum(output_term, ("lat", "lon"))
    sum_squares = jnp.sum(summed * summed)
    clip_factor = jnp.minimum(
        jnp.float32(1.0), jnp.float32(model_width) / (jnp.sqrt(sum_squares) + 1e-06)
    )
    d_output = summed * clip_factor
    return (d_tokens, d_output)


def solution(mesh):
    placed = (P("lat", "lon", None), P("lat", "lon", None), P(), P(), P(), P())
    return jax.shard_map(
        per_device,
        mesh=mesh,
        in_specs=placed,
        out_specs=(P("lat", "lon", None), P()),
        check_vma=False,
    )
```

profile of v0, /device:TPU:1, one launch (start us, length us, event | category | flops | bytes accessed | tf_op | source)
XLA Modules:
  0.0 523.2 jit_solution(18081679179539536854)
XLA Ops:
  7.2 0.0 copy-start
  7.2 0.0 copy-start.2
  7.2 0.0 all-reduce.2.cloned.1.call-start
  7.2 1.0 fusion.20
  8.3 7.9 %collective-permute-start.2 = (bf16[6,12,512]{2,1,0:T(8,128)(2,1)S(1)}, bf16[6,12,512]{2,1,0:T(8,128)(2,1)S(1)}, u32[]{:S(2)}, u32[]{:S(2)}) collective-permute-start(bf16[6,12,512]{2,1,0:T(8,128)(2,1)S(1)} %get-tuple-element.11), channel_id=1, source_target_pairs={{0,448},{64,0},{128,64},{192,128},{256,192},{320,256},{384,320},{4... | collective-permute-start | bytes 221192 | tf_op jit(solution)/shard_map/ppermute | solution.py:16
  16.2 1.0 fusion.19
  17.2 2.1 collective-permute-start
  19.3 0.1 broadcast_in_dim.14
  19.4 0.1 eq.21
  19.5 0.1 broadcast_compare_fusion
  19.6 1.1 constant_dynamic-update-slice_fusion.2
  20.7 1.1 constant_dynamic-update-slice_fusion.1
  21.8 0.0 copy-done.2
  21.8 0.0 collective-permute-done.2
  21.9 3.2 collective-permute-start.3
  25.1 0.0 collective-permute-done
  25.2 11.1 %collective-permute-start.1 = (bf16[12,6,512]{2,1,0:T(8,128)(2,1)S(1)}, bf16[12,6,512]{2,1,0:T(8,128)(2,1)S(1)}, u32[]{:S(2)}, u32[]{:S(2)}) collective-permute-start(bf16[12,6,512]{2,1,0:T(8,128)(2,1)S(1)} %get-tuple-element.5), channel_id=1, source_target_pairs={{0,63},{1,0},{2,1},{3,2},{4,3},{5,4},{6,5},{7,6},{8,7},{9,8},{10,9... | collective-permute-start | bytes 221192 | tf_op jit(solution)/shard_map/ppermute | solution.py:16
  36.3 0.0 collective-permute-done.3
  36.3 0.1 pad_maximum_fusion.3
  36.4 0.0 copy-done
  36.4 0.3 convolution_convert_fusion.6
  36.8 0.8 copy.18
  37.6 0.0 collective-permute-done.1
  37.6 0.1 pad_maximum_fusion.2
  37.7 0.4 convolution_convert_fusion
  38.1 0.3 copy.17
  38.4 0.0 copy-start.3
  38.4 2.4 fusion.21
  40.8 0.0 copy-done.3
  40.8 0.0 copy-start.1
  40.8 2.3 fusion.7
  43.2 0.1 copy-done.1
  43.2 0.6 multiply_reduce_fusion
  43.8 0.5 multiply_convert_fusion
  44.3 0.5 fusion.6
  44.8 0.3 fusion.5
  45.1 1.1 convolution_convert_fusion.1
  46.2 0.0 copy-start.4
  46.2 0.2 pad_maximum_fusion
  46.4 0.7 convolution_convert_fusion.5
  47.1 0.0 copy-done.4
  47.1 1.3 fusion.22
  48.4 0.0 all-reduce.2.cloned.1.call-update
  48.5 1.9 collective-permute-start.4
  50.4 2.9 collective-permute-done.4
  53.3 4.4 collective-permute-start.5
  57.7 4.6 collective-permute-done.5
  62.3 0.7 fusion.12
  63.0 448.3 %all-reduce.2.cloned.1.call-done = f32[512,512]{1,0:T(8,128)} async-done(((f32[512,512]{1,0:T(8,128)}), f32[512,512]{1,0:T(8,128)}) %all-reduce.2.cloned.1.call-update) | async-done | bytes 1048592 | tf_op jit(solution)/shard_map/psum | solution.py:116
  511.3 2.1 multiply_reduce_fusion.1
  514.1 2.3 broadcast_multiply_fusion
  (9 shorter events, 0.3 us)
Async XLA Ops:
  7.2 29.3 %copy-start = (bf16[512,512]{1,0:T(8,128)(2,1)S(1)}, bf16[512,512]{1,0:T(8,128)(2,1)}, u32[]{:S(2)}) copy-start(bf16[512,512]{1,0:T(8,128)(2,1)} %param.11) | copy-start | bytes 1572868
  7.2 14.6 %copy-start.2 = (bf16[512,512]{1,0:T(8,128)(2,1)S(1)}, bf16[512,512]{1,0:T(8,128)(2,1)}, u32[]{:S(2)}) copy-start(bf16[512,512]{1,0:T(8,128)(2,1)} %param.10) | copy-start | bytes 1572868
  7.2 504.1 %all-reduce.2.cloned.1.call-start = ((), (), s32[]{:S(2)}) async-start(), calls=%async_computation | async-start | bytes 2097152 | tf_op jit(solution)/shard_map/psum | solution.py:116
  8.3 13.5 %collective-permute-start.2 = (bf16[6,12,512]{2,1,0:T(8,128)(2,1)S(1)}, bf16[6,12,512]{2,1,0:T(8,128)(2,1)S(1)}, u32[]{:S(2)}, u32[]{:S(2)}) collective-permute-start(bf16[6,12,512]{2,1,0:T(8,128)(2,1)S(1)} %get-tuple-element.11), channel_id=1, source_target_pairs={{0,448},{64,0},{128,64},{192,128},{256,192},{320,256},{384,320},{4... | collective-permute-start | bytes 221192 | tf_op jit(solution)/shard_map/ppermute | solution.py:16
  17.2 8.0 %collective-permute-start = (bf16[6,12,512]{2,1,0:T(8,128)(2,1)S(1)}, bf16[6,12,512]{2,1,0:T(8,128)(2,1)S(1)}, u32[]{:S(2)}, u32[]{:S(2)}) collective-permute-start(bf16[6,12,512]{2,1,0:T(8,128)(2,1)S(1)} %get-tuple-element.7), channel_id=1, source_target_pairs={{0,448},{64,0},{128,64},{192,128},{256,192},{320,256},{384,320},{4... | collective-permute-start | bytes 221192 | tf_op jit(solution)/shard_map/ppermute | solution.py:16
  21.9 14.4 %collective-permute-start.3 = (bf16[12,6,512]{2,1,0:T(8,128)(2,1)S(1)}, bf16[12,6,512]{2,1,0:T(8,128)(2,1)S(1)}, u32[]{:S(2)}, u32[]{:S(2)}) collective-permute-start(bf16[12,6,512]{2,1,0:T(8,128)(2,1)S(1)} %get-tuple-element.9), channel_id=1, source_target_pairs={{0,63},{1,0},{2,1},{3,2},{4,3},{5,4},{6,5},{7,6},{8,7},{9,8},{10,9... | collective-permute-start | bytes 221192 | tf_op jit(solution)/shard_map/ppermute | solution.py:16
  25.2 12.4 %collective-permute-start.1 = (bf16[12,6,512]{2,1,0:T(8,128)(2,1)S(1)}, bf16[12,6,512]{2,1,0:T(8,128)(2,1)S(1)}, u32[]{:S(2)}, u32[]{:S(2)}) collective-permute-start(bf16[12,6,512]{2,1,0:T(8,128)(2,1)S(1)} %get-tuple-element.5), channel_id=1, source_target_pairs={{0,63},{1,0},{2,1},{3,2},{4,3},{5,4},{6,5},{7,6},{8,7},{9,8},{10,9... | collective-permute-start | bytes 221192 | tf_op jit(solution)/shard_map/ppermute | solution.py:16
  38.4 2.4 copy-start.3
  40.8 2.4 copy-start.1
  46.2 0.9 copy-start.4
  48.5 4.8 collective-permute-start.4
  53.3 9.0 %collective-permute-start.5 = (bf16[6,12,512]{2,1,0:T(8,128)(2,1)S(1)}, bf16[6,12,512]{2,1,0:T(8,128)(2,1)S(1)}, u32[]{:S(2)}, u32[]{:S(2)}) collective-permute-start(bf16[6,12,512]{2,1,0:T(8,128)(2,1)S(1)} %fusion.13), channel_id=1, source_target_pairs={{0,64},{64,128},{128,192},{192,256},{256,320},{320,384},{384,448},... | collective-permute-start | bytes 221192 | tf_op jit(solution)/shard_map/ppermute | solution.py:16
Sparse Core Ops, SparseCore 0:
  48.5 462.6 all-reduce.1
where the time goes:
time: 524 us; the launch traced here: 523 us
  waiting for transfers between devices  456 us (87%)
  starting transfers between devices  30.8 us (6%)
  between operations  15 us (3%)
  matrix products  9.76 us (2%)
  other arithmetic  6.19 us (1%)
  local copies, waits for them, and re-layouts  5.73 us (1%)
    psum x1, waiting for transfers between devices, per_device(): summed = lax.psum(output_term, ('lat', 'lon'))  448 us
    ppermute x6, starting transfers between devices, from_behind(): return lax.ppermute(value, axis, pairs)  30.7 us
  transfers between devices with their start and end apart: 7, of which 3 were waited for; matrix products, arithmetic and copies ran while one was open for 1% of the time, Pallas kernels for 0%

commit v1 on v0

v1 whole, which is shorter than its diff:
```python
import math

import jax
import jax.numpy as jnp
from jax import lax
from jax.experimental import pallas as pl
from jax.experimental.pallas import tpu as pltpu
from jax.sharding import Mesh
from jax.sharding import PartitionSpec as P

HEADS = 16
DH = 32
D = 512
HALF = 6
QUAD = HALF * HALF
N = 4 * QUAD
SPLIT = ("y", "xh", "z", "xl", "core")
LAT = ("y", "xh")
LON = ("z", "xl", "core")
PLANE = ("y", "xh", "xl", "core")
F32 = jnp.float32
BF16 = jnp.bfloat16
NT = (((1,), (1,)), ((), ()))
VMEM = pl.BlockSpec(memory_space=pltpu.VMEM)
SMEM = pl.BlockSpec(memory_space=pltpu.SMEM)
PARAMS = pltpu.CompilerParams(vmem_limit_bytes=40 * 1024 * 1024)


def dot(a, b, dims=(((1,), (0,)), ((), ()))):
    return lax.dot_general(a, b, dims, preferred_element_type=F32)


def window_kernel(
    last_ref, tok_ref, cot_ref, lon_ref, lat_ref, diag_ref, wq_ref, wk_ref, wv_ref, wo_ref,
    g_ref, own_out, lon_out, lat_out, diag_out,
    x_s, c_s, ot_s, dqt_s, dkt_s, dvt_s, dr_s,
):
    for i in range(HALF):
        x_s[HALF * i : HALF * (i + 1), :] = tok_ref[HALF + i].astype(F32)[HALF:]
        c_s[HALF * i : HALF * (i + 1), :] = cot_ref[HALF + i].astype(F32)[HALF:]
        for part, ref in ((1, lon_ref), (2, lat_ref), (3, diag_ref)):
            at = QUAD * part + HALF * i
            x_s[at : at + HALF, :] = ref[0, i].astype(F32)
            c_s[at : at + HALF, :] = ref[1, i].astype(F32)
    x = x_s[...].astype(BF16)
    c = c_s[...].astype(BF16)
    q = dot(x, wq_ref[...]).astype(BF16)
    k = dot(x, wk_ref[...]).astype(BF16)
    v = dot(x, wv_ref[...]).astype(BF16)
    dot_t = dot(wo_ref[...], c, NT).astype(BF16)
    qt = q.T
    kt = k.T
    vt = v.T
    factor = 1.0 / math.sqrt(DH)
    row = lax.broadcasted_iota(jnp.int32, (N, N), 0) >= 2 * QUAD
    col = lax.broadcasted_iota(jnp.int32, (N, N), 1) >= 2 * QUAD
    bias = jnp.where(jnp.logical_and(row != col, last_ref[0] == 1), F32(-1e30), F32(0.0))
    for h in range(HEADS):
        at = slice(DH * h, DH * (h + 1))
        kh, vh = k[:, at], v[:, at]
        qth, kth, vth, doth = qt[at], kt[at], vt[at], dot_t[at]
        s = dot(kh, qth) * factor + bias
        e = jnp.exp(s - jnp.max(s, axis=0, keepdims=True))
        p = e * (1.0 / jnp.sum(e, axis=0, keepdims=True))
        pb = p.astype(BF16)
        ot_s[at, :] = dot(vth, pb).astype(BF16)
        dp = dot(vh, doth)
        dvt_s[at, :] = dot(doth, pb, NT).astype(BF16)
        inner = jnp.sum(p * dp, axis=0, keepdims=True)
        ds = (factor * p * (dp - inner)).astype(BF16)
        dqt_s[at, :] = dot(kth, ds).astype(BF16)
        dkt_s[at, :] = dot(qth, ds, NT).astype(BF16)
    g_ref[...] = dot(ot_s[...], c).astype(BF16)
    dr_s[...] = (
        dot(dqt_s[...].T, wq_ref[...], NT)
        + dot(dkt_s[...].T, wk_ref[...], NT)
        + dot(dvt_s[...].T, wv_ref[...], NT)
    )
    for part, ref in enumerate((own_out, lon_out, lat_out, diag_out)):
        for i in range(HALF):
            at = QUAD * part + HALF * i
            ref[i] = dr_s[at : at + HALF, :].astype(BF16)


def window_call(last, tokens, cotangent, lon, lat, diag, wq, wk, wv, wo):
    quad = jax.ShapeDtypeStruct((HALF, HALF, D), BF16)
    return pl.pallas_call(
        window_kernel,
        out_shape=(jax.ShapeDtypeStruct((D, D), BF16), quad, quad, quad, quad),
        in_specs=[SMEM] + [VMEM] * 9,
        out_specs=(VMEM,) * 5,
        scratch_shapes=[
            pltpu.VMEM((N, D), F32),
            pltpu.VMEM((N, D), F32),
            pltpu.VMEM((D, N), BF16),
            pltpu.VMEM((D, N), BF16),
            pltpu.VMEM((D, N), BF16),
            pltpu.VMEM((D, N), BF16),
            pltpu.VMEM((N, D), F32),
        ],
        compiler_params=PARAMS,
    )(last, tokens, cotangent, lon, lat, diag, wq, wk, wv, wo)


def sum_kernel(in_ref, out_ref):
    total = in_ref[0].astype(F32)
    for i in range(1, in_ref.shape[0]):
        total = total + in_ref[i].astype(F32)
    total = total.astype(BF16)
    for i in range(out_ref.shape[0]):
        out_ref[i] = total


def sum_and_repeat(parts, copies):
    return pl.pallas_call(
        sum_kernel,
        out_shape=jax.ShapeDtypeStruct((copies,) + parts.shape[1:], BF16),
        in_specs=[VMEM],
        out_specs=VMEM,
        compiler_params=PARAMS,
    )(parts)


def finish_kernel(g_ref, own_ref, lon_ref, lat_ref, diag_ref, dtok_ref, dout_ref):
    g = g_ref[...].astype(F32)
    norm = jnp.sqrt(jnp.sum(g * g, keepdims=True))
    dout_ref[...] = g * jnp.minimum(F32(1.0), F32(D) / (norm + 1e-6))
    for i in range(HALF):
        top = (diag_ref[i].astype(F32), lat_ref[i].astype(F32))
        dtok_ref[i] = jnp.concatenate(top, axis=0).astype(BF16)
        bottom = (lon_ref[i].astype(F32), own_ref[i].astype(F32))
        dtok_ref[HALF + i] = jnp.concatenate(bottom, axis=0).astype(BF16)


def finish_call(g, own, lon, lat, diag):
    return pl.pallas_call(
        finish_kernel,
        out_shape=(
            jax.ShapeDtypeStruct((2 * HALF, 2 * HALF, D), BF16),
            jax.ShapeDtypeStruct((D, D), F32),
        ),
        in_specs=[VMEM] * 5,
        out_specs=(VMEM, VMEM),
        compiler_params=PARAMS,
    )(g, own, lon, lat, diag)


def shifted(value, lat_step, lon_step):
    axes = (LAT if lat_step else ()) + (LON if lon_step else ())
    n_lat = lax.axis_size(LAT) if lat_step else 1
    n_lon = lax.axis_size(LON) if lon_step else 1
    pairs = []
    for a in range(n_lat):
        for b in range(n_lon):
            to = (a + lat_step) % n_lat * n_lon + (b + lon_step) % n_lon
            pairs.append((a * n_lon + b, to))
    return lax.ppermute(value, axes, pairs)


def per_device(tokens, cotangent, w_query, w_key, w_value, w_output):
    lat = shifted(jnp.stack([tokens[:HALF, HALF:], cotangent[:HALF, HALF:]]), -1, 0)
    lon = shifted(jnp.stack([tokens[HALF:, :HALF], cotangent[HALF:, :HALF]]), 0, -1)
    diag = shifted(jnp.stack([tokens[:HALF, :HALF], cotangent[:HALF, :HALF]]), -1, -1)
    last = (lax.axis_index(LAT) == lax.axis_size(LAT) - 1).astype(jnp.int32).reshape(1)
    g, own, lon, lat, diag = window_call(
        last, tokens, cotangent, lon, lat, diag, w_query, w_key, w_value, w_output
    )
    lat = shifted(lat, 1, 0)
    lon = shifted(lon, 0, 1)
    diag = shifted(diag, 1, 1)
    n_plane = lax.axis_size(PLANE)
    n_z = lax.axis_size("z")
    parts = g.reshape(n_plane, D // n_plane, D)
    parts = lax.all_to_all(parts, PLANE, 0, 0, tiled=True)
    parts = lax.all_to_all(sum_and_repeat(parts, n_z), "z", 0, 0, tiled=True)
    parts = lax.all_to_all(sum_and_repeat(parts, n_plane), PLANE, 0, 0, tiled=True)
    return finish_call(parts.reshape(D, D), own, lon, lat, diag)


def solution(mesh):
    fine = Mesh(mesh.devices.reshape(4, 2, 16, 2, 2), SPLIT)
    tiles = P(LAT, LON, None)
    return jax.shard_map(
        per_device,
        mesh=fine,
        in_specs=(tiles, tiles, P(), P(), P(), P()),
        out_specs=(tiles, P()),
        check_vma=False,
    )
```

time: 524 us -> 105 us (0.20)
  waiting for transfers between devices: 456 us -> 7.34 us
  blocking collectives: 0 us -> 39 us
  between operations: 15 us -> 0.79 us
  starting transfers between devices: 30.8 us -> 42.9 us
  Pallas kernels: 0 us -> 10.5 us
  matrix products: 9.76 us -> 0 us
  other arithmetic: 6.19 us -> 0.07 us
    psum x1 -> x0, waiting for transfers between devices: 448 us -> none  [per_device(): summed = lax.psum(output_term, ('lat', 'lon'))]
    all_to_all x0 -> x2, blocking collectives: none -> 39 us  [the longest x1 19.8 us: per_device(): parts = lax.all_to_all(sum_and_repeat(parts, n_z), 'z', 0, 0, tiled=True)]
    pallas_call x0 -> x4, Pallas kernels: none -> 10.5 us  [the longest x1 8.07 us: window_call(): pl.pallas_call(window_kernel, out_shape=(jax.ShapeDtypeStruct((D, D), BF1...]
    all_to_all x0 -> x1, starting transfers between devices: none -> 8.91 us  [per_device(): lax.all_to_all(sum_and_repeat(parts, n_plane), PLANE, 0, 0, tiled=True)]
    dot_general x9 -> x0, matrix products: 7.34 us -> none  [the longest x1 2.3 us: window_backward(): jnp.einsum('whqk,wqhd->wkhd', probs_low, d_attended, preferred_element_ty...]
  transfers between devices with their start and end apart: 7 -> 7, of which waited for: 3 -> 3; matrix products, arithmetic and copies ran while one was open for 1% -> 0% of each run, Pallas kernels for 0% -> 0%
where the time goes in v1:
time: 105 us
  starting transfers between devices  42.9 us (41%)
  blocking collectives  39 us (37%)
  Pallas kernels  10.5 us (10%)
  waiting for transfers between devices  7.34 us (7%)
  local copies, waits for them, and re-layouts  4.25 us (4%)
    ppermute x6, starting transfers between devices, shifted(): return lax.ppermute(value, axes, pairs)  33.9 us
    all_to_all x1, blocking collectives, per_device(): parts = lax.all_to_all(sum_and_repeat(parts, n_z), 'z', 0, 0, tiled=True)  19.8 us
    all_to_all x1, blocking collectives, per_device(): parts = lax.all_to_all(parts, PLANE, 0, 0, tiled=True)  19.2 us
    all_to_all x1, starting transfers between devices, per_device(): lax.all_to_all(sum_and_repeat(parts, n_plane), PLANE, 0, 0, tiled=True)  8.91 us
    pallas_call x1, Pallas kernels, window_call(): pl.pallas_call(window_kernel, out_shape=(jax.ShapeDtypeStruct((D, D), BF1...  8.07 us
    ppermute x6, waiting for transfers between devices, shifted(): return lax.ppermute(value, axes, pairs)  7.34 us
    unnamed x12, local copies, waits for them, and re-layouts  3.14 us
  transfers between devices with their start and end apart: 7, of which 3 were waited for; matrix products, arithmetic and copies ran while one was open for 0% of the time, Pallas kernels for 0%

profile of v1, /device:TPU:1, one launch (start us, length us, event | category | flops | bytes accessed | tf_op | source)
XLA Modules:
  0.0 104.7 jit_solution(1675384490872673289)
XLA Ops:
  0.6 0.0 copy-start.2
  0.6 1.1 %slice_bitcast_fusion = (bf16[1,6,6,512]{3,2,1,0:T(8,128)(2,1)S(1)}, bf16[1,6,6,512]{3,2,1,0:T(8,128)(2,1)S(1)}, bf16[1,6,6,512]{3,2,1,0:T(8,128)(2,1)S(1)}, bf1...) fusion(bf16[12,12,512]{2,1,0:T(8,128)(2,1)} %cot_ref.1, ...), kind=kLoop, calls=%fused_computation.3 | loop fusion | bytes 442368 | tf_op jit(solution)/shard_map/stack | solution.py:163
  1.8 8.8 %collective-permute-start = (bf16[2,6,6,512]{3,2,1,0:T(8,128)(2,1)S(1)}, bf16[2,6,6,512]{3,2,1,0:T(8,128)(2,1)S(1)}, u32[]{:S(2)}, u32[]{:S(2)}) collective-permute-start(bf16[2,6,6,512]{3,2,1,0:T(8,128)(2,1)S(1)} %pad_maximum_fusion), channel_id=1, source_target_pairs={{0,63},{1,0},{2,1},{3,2},{4,3},{5,4},{6,5},{7,6},{8,7},{9,8},{10,9... | collective-permute-start | bytes 221192 | tf_op jit(solution)/shard_map/ppermute | solution.py:157
  10.6 0.0 copy-start
  10.6 0.0 copy-start.1
  10.6 2.1 %collective-permute-start.1 = (bf16[2,6,6,512]{3,2,1,0:T(8,128)(2,1)S(1)}, bf16[2,6,6,512]{3,2,1,0:T(8,128)(2,1)S(1)}, u32[]{:S(2)}, u32[]{:S(2)}) collective-permute-start(bf16[2,6,6,512]{3,2,1,0:T(8,128)(2,1)S(1)} %pad_maximum_fusion.1), channel_id=1, source_target_pairs={{0,448},{64,0},{128,64},{192,128},{256,192},{320,256},{384,320},{4... | collective-permute-start | bytes 221192 | tf_op jit(solution)/shard_map/ppermute | solution.py:157
  12.7 12.0 %collective-permute-start.2 = (bf16[2,6,6,512]{3,2,1,0:T(8,128)(2,1)S(1)}, bf16[2,6,6,512]{3,2,1,0:T(8,128)(2,1)S(1)}, u32[]{:S(2)}, u32[]{:S(2)}) collective-permute-start(bf16[2,6,6,512]{3,2,1,0:T(8,128)(2,1)S(1)} %pad_maximum_fusion.2), channel_id=1, source_target_pairs={{0,511},{1,448},{2,449},{3,450},{4,451},{5,452},{6,453},{7,454},{8... | collective-permute-start | bytes 221192 | tf_op jit(solution)/shard_map/ppermute | solution.py:157
  24.7 0.0 collective-permute-done.lon_ref
  24.7 0.0 collective-permute-done.1.lat_ref
  24.7 1.6 %collective-permute-done.2.diag_ref = bf16[2,6,6,512]{3,2,1,0:T(8,128)(2,1)S(1)} collective-permute-done((bf16[2,6,6,512]{3,2,1,0:T(8,128)(2,1)S(1)}, bf16[2,6,6,512]{3,2,1,0:T(8,128)(2,1)S(1)}, u32[]{:S(2)}, u32[]{:S(2)}) %collective-permute-start.2) | collective-permute-done | bytes 73760 | tf_op jit(solution)/shard_map/ppermute | solution.py:157
  26.3 0.0 copy-done.2
  26.3 0.0 copy-done
  26.3 0.0 copy-done.1
  26.3 0.0 copy-start.3
  26.3 1.0 copy-done.3
  27.4 0.0 copy-start.4
  27.4 1.0 copy-done.4
  28.4 0.0 copy-start.5
  28.4 1.0 copy-done.5
  29.5 8.1 %shard_map.77 = (bf16[512,512]{1,0:T(8,128)(2,1)S(1)}, bf16[6,6,512]{2,1,0:T(8,128)(2,1)S(1)}, bf16[6,6,512]{2,1,0:T(8,128)(2,1)S(1)}, bf16[6,6,512]{2,1,0:T(8,128)(2,1)S(1)}, bf16[6,6,512]{2,1,0:T(8,128)(2,1)S(1)}) custom-call(s32[1]{0:T(128)} %bitcast.last_ref, bf16[12,12,512]{2,1,0:T(8,128)(2,1)S(1)} %copy-done, bf16[12,12,512]{2,1,0:T(8,128)(2,1)S(1)} %copy-done.1, ...), custom_call_target="tpu_custom_call" | custom-call | tf_op jit(solution)/shard_map/pallas_call | solution.py:87
  37.5 19.2 %all_to_all.15.in_ref = bf16[32,16,512]{2,1,0:T(8,128)(2,1)S(1)} all-to-all(bf16[32,16,512]{2,1,0:T(8,128)(2,1)S(1)} %bitcast.16), channel_id=1, replica_groups=mesh['y'=4,'xh'=2,'z'=16,'xl'=2,'core'=2] {'y','xh','xl','core'}, dimensions={0} | all-to-all | bytes 1048576 | tf_op jit(solution)/shard_map/all_to_all | solution.py:174
  56.7 0.1 shard_map.78
  56.8 19.8 %all_to_all.16.in_ref = bf16[16,16,512]{2,1,0:T(8,128)(2,1)S(1)} all-to-all(bf16[16,16,512]{2,1,0:T(8,128)(2,1)S(1)} %shard_map.78), channel_id=1, replica_groups=mesh['y'=4,'xh'=2,'z'=16,'xl'=2,'core'=2] {'z'}, dimensions={0} | all-to-all | bytes 524288 | tf_op jit(solution)/shard_map/all_to_all | solution.py:175
  76.6 0.9 shard_map.79
  77.5 8.9 %all-to-all-start.2 = ((bf16[32,16,512]{2,1,0:T(8,128)(2,1)}), bf16[32,16,512]{2,1,0:T(8,128)(2,1)S(1)}, u32[]{:S(2)}, u32[]{:S(2)}) async-start(bf16[32,16,512]{2,1,0:T(8,128)(2,1)} %shard_map.79), calls=%async_computation.2 | async-start | bytes 1048576 | tf_op jit(solution)/shard_map/all_to_all | solution.py:176
  86.4 3.5 %collective-permute-start.3 = (bf16[6,6,512]{2,1,0:T(8,128)(2,1)S(1)}, bf16[6,6,512]{2,1,0:T(8,128)(2,1)S(1)}, u32[]{:S(2)}, u32[]{:S(2)}) collective-permute-start(bf16[6,6,512]{2,1,0:T(8,128)(2,1)S(1)} %get-tuple-element.9), channel_id=1, source_target_pairs={{0,1},{1,2},{2,3},{3,4},{4,5},{5,6},{6,7},{7,8},{8,9},{9,10},{10,1... | collective-permute-start | bytes 110600 | tf_op jit(solution)/shard_map/ppermute | solution.py:157
  89.9 4.3 %collective-permute-start.4 = (bf16[6,6,512]{2,1,0:T(8,128)(2,1)S(1)}, bf16[6,6,512]{2,1,0:T(8,128)(2,1)S(1)}, u32[]{:S(2)}, u32[]{:S(2)}) collective-permute-start(bf16[6,6,512]{2,1,0:T(8,128)(2,1)S(1)} %get-tuple-element.10), channel_id=1, source_target_pairs={{0,64},{64,128},{128,192},{192,256},{256,320},{320,384},{384,448},... | collective-permute-start | bytes 110600 | tf_op jit(solution)/shard_map/ppermute | solution.py:157
  94.3 3.3 %collective-permute-start.5 = (bf16[6,6,512]{2,1,0:T(8,128)(2,1)S(1)}, bf16[6,6,512]{2,1,0:T(8,128)(2,1)S(1)}, u32[]{:S(2)}, u32[]{:S(2)}) collective-permute-start(bf16[6,6,512]{2,1,0:T(8,128)(2,1)S(1)} %get-tuple-element.11), channel_id=1, source_target_pairs={{0,65},{1,66},{2,67},{3,68},{4,69},{5,70},{6,71},{7,72},{8,73},{9,... | collective-permute-start | bytes 110600 | tf_op jit(solution)/shard_map/ppermute | solution.py:157
  97.5 0.0 collective-permute-done.3.lon_ref
  97.6 2.5 %collective-permute-done.4.lat_ref = bf16[6,6,512]{2,1,0:T(8,128)(2,1)S(1)} collective-permute-done((bf16[6,6,512]{2,1,0:T(8,128)(2,1)S(1)}, bf16[6,6,512]{2,1,0:T(8,128)(2,1)S(1)}, u32[]{:S(2)}, u32[]{:S(2)}) %collective-permute-start.4) | collective-permute-done | bytes 36896 | tf_op jit(solution)/shard_map/ppermute | solution.py:157
  100.1 3.2 %collective-permute-done.5.diag_ref = bf16[6,6,512]{2,1,0:T(8,128)(2,1)S(1)} collective-permute-done((bf16[6,6,512]{2,1,0:T(8,128)(2,1)S(1)}, bf16[6,6,512]{2,1,0:T(8,128)(2,1)S(1)}, u32[]{:S(2)}, u32[]{:S(2)}) %collective-permute-start.5) | collective-permute-done | bytes 36896 | tf_op jit(solution)/shard_map/ppermute | solution.py:157
  103.3 0.0 all-to-all-done.2
  103.3 1.4 %shard_map.80 = (bf16[12,12,512]{2,1,0:T(8,128)(2,1)}, f32[512,512]{1,0:T(8,128)}) custom-call(bf16[512,512]{1,0:T(8,128)(2,1)S(1)} %bitcast.15, bf16[6,6,512]{2,1,0:T(8,128)(2,1)S(1)} %get-tuple-element.8.own_ref, bf16[6,6,512]{2,1,0:T(8,128)(2,1)S(1)} %collective-permute-done.3.lon_ref, bf16[6,6,512]{2,1,0:T(8,128)(2,1)S(1)} %collective-permute-done.4.lat_ref, ...), custom_call_target="tpu_custom_call" | custom-call | tf_op jit(solution)/shard_map/pallas_call | solution.py:136
  (3 shorter events, 0.1 us)
Async XLA Ops:
  0.6 25.7 %copy-start.2 = (bf16[512,512]{1,0:T(8,128)(2,1)S(1)}, bf16[512,512]{1,0:T(8,128)(2,1)}, u32[]{:S(2)}) copy-start(bf16[512,512]{1,0:T(8,128)(2,1)} %wq_ref.1) | copy-start | bytes 1572868
  1.8 22.9 %collective-permute-start = (bf16[2,6,6,512]{3,2,1,0:T(8,128)(2,1)S(1)}, bf16[2,6,6,512]{3,2,1,0:T(8,128)(2,1)S(1)}, u32[]{:S(2)}, u32[]{:S(2)}) collective-permute-start(bf16[2,6,6,512]{3,2,1,0:T(8,128)(2,1)S(1)} %pad_maximum_fusion), channel_id=1, source_target_pairs={{0,63},{1,0},{2,1},{3,2},{4,3},{5,4},{6,5},{7,6},{8,7},{9,8},{10,9... | collective-permute-start | bytes 221192 | tf_op jit(solution)/shard_map/ppermute | solution.py:157
  10.6 15.7 %copy-start = (bf16[12,12,512]{2,1,0:T(8,128)(2,1)S(1)}, bf16[12,12,512]{2,1,0:T(8,128)(2,1)}, u32[]{:S(2)}) copy-start(bf16[12,12,512]{2,1,0:T(8,128)(2,1)} %tok_ref.1) | copy-start | bytes 442372
  10.6 15.7 %copy-start.1 = (bf16[12,12,512]{2,1,0:T(8,128)(2,1)S(1)}, bf16[12,12,512]{2,1,0:T(8,128)(2,1)}, u32[]{:S(2)}) copy-start(bf16[12,12,512]{2,1,0:T(8,128)(2,1)} %cot_ref.1) | copy-start | bytes 442372
  10.6 14.1 %collective-permute-start.1 = (bf16[2,6,6,512]{3,2,1,0:T(8,128)(2,1)S(1)}, bf16[2,6,6,512]{3,2,1,0:T(8,128)(2,1)S(1)}, u32[]{:S(2)}, u32[]{:S(2)}) collective-permute-start(bf16[2,6,6,512]{3,2,1,0:T(8,128)(2,1)S(1)} %pad_maximum_fusion.1), channel_id=1, source_target_pairs={{0,448},{64,0},{128,64},{192,128},{256,192},{320,256},{384,320},{4... | collective-permute-start | bytes 221192 | tf_op jit(solution)/shard_map/ppermute | solution.py:157
  12.7 13.6 %collective-permute-start.2 = (bf16[2,6,6,512]{3,2,1,0:T(8,128)(2,1)S(1)}, bf16[2,6,6,512]{3,2,1,0:T(8,128)(2,1)S(1)}, u32[]{:S(2)}, u32[]{:S(2)}) collective-permute-start(bf16[2,6,6,512]{3,2,1,0:T(8,128)(2,1)S(1)} %pad_maximum_fusion.2), channel_id=1, source_target_pairs={{0,511},{1,448},{2,449},{3,450},{4,451},{5,452},{6,453},{7,454},{8... | collective-permute-start | bytes 221192 | tf_op jit(solution)/shard_map/ppermute | solution.py:157
  26.3 1.0 copy-start.3
  27.4 1.0 copy-start.4
  28.4 1.0 copy-start.5
  77.5 25.8 %all-to-all-start.2 = ((bf16[32,16,512]{2,1,0:T(8,128)(2,1)}), bf16[32,16,512]{2,1,0:T(8,128)(2,1)S(1)}, u32[]{:S(2)}, u32[]{:S(2)}) async-start(bf16[32,16,512]{2,1,0:T(8,128)(2,1)} %shard_map.79), calls=%async_computation.2 | async-start | bytes 1048576 | tf_op jit(solution)/shard_map/all_to_all | solution.py:176
  86.4 11.2 %collective-permute-start.3 = (bf16[6,6,512]{2,1,0:T(8,128)(2,1)S(1)}, bf16[6,6,512]{2,1,0:T(8,128)(2,1)S(1)}, u32[]{:S(2)}, u32[]{:S(2)}) collective-permute-start(bf16[6,6,512]{2,1,0:T(8,128)(2,1)S(1)} %get-tuple-element.9), channel_id=1, source_target_pairs={{0,1},{1,2},{2,3},{3,4},{4,5},{5,6},{6,7},{7,8},{8,9},{9,10},{10,1... | collective-permute-start | bytes 110600 | tf_op jit(solution)/shard_map/ppermute | solution.py:157
  89.9 10.1 %collective-permute-start.4 = (bf16[6,6,512]{2,1,0:T(8,128)(2,1)S(1)}, bf16[6,6,512]{2,1,0:T(8,128)(2,1)S(1)}, u32[]{:S(2)}, u32[]{:S(2)}) collective-permute-start(bf16[6,6,512]{2,1,0:T(8,128)(2,1)S(1)} %get-tuple-element.10), channel_id=1, source_target_pairs={{0,64},{64,128},{128,192},{192,256},{256,320},{320,384},{384,448},... | collective-permute-start | bytes 110600 | tf_op jit(solution)/shard_map/ppermute | solution.py:157
  94.3 9.0 %collective-permute-start.5 = (bf16[6,6,512]{2,1,0:T(8,128)(2,1)S(1)}, bf16[6,6,512]{2,1,0:T(8,128)(2,1)S(1)}, u32[]{:S(2)}, u32[]{:S(2)}) collective-permute-start(bf16[6,6,512]{2,1,0:T(8,128)(2,1)S(1)} %get-tuple-element.11), channel_id=1, source_target_pairs={{0,65},{1,66},{2,67},{3,68},{4,69},{5,70},{6,71},{7,72},{8,73},{9,... | collective-permute-start | bytes 110600 | tf_op jit(solution)/shard_map/ppermute | solution.py:157

commit v2 on v1

--- a/solution.py
+++ b/solution.py
@@ -12,6 +12,7 @@
 DH = 32
 D = 512
 HALF = 6
+FACTOR = 1.0 / math.sqrt(DH)
 QUAD = HALF * HALF
 N = 4 * QUAD
 SPLIT = ("y", "xh", "z", "xl", "core")
@@ -22,18 +23,57 @@
 BF16 = jnp.bfloat16
 NT = (((1,), (1,)), ((), ()))
 VMEM = pl.BlockSpec(memory_space=pltpu.VMEM)
+ANY = pl.BlockSpec(memory_space=pl.ANY)
+HBM = pl.BlockSpec(memory_space=pltpu.HBM)
 SMEM = pl.BlockSpec(memory_space=pltpu.SMEM)
-PARAMS = pltpu.CompilerParams(vmem_limit_bytes=40 * 1024 * 1024)
+MIB = 1024 * 1024
+PARAMS = pltpu.CompilerParams(vmem_limit_bytes=12 * MIB)
+WIDE = pltpu.CompilerParams(vmem_limit_bytes=52 * MIB)
 
 
 def dot(a, b, dims=(((1,), (0,)), ((), ()))):
     return lax.dot_general(a, b, dims, preferred_element_type=F32)
 
 
-def window_kernel(
-    last_ref, tok_ref, cot_ref, lon_ref, lat_ref, diag_ref, wq_ref, wk_ref, wv_ref, wo_ref,
-    g_ref, own_out, lon_out, lat_out, diag_out,
-    x_s, c_s, ot_s, dqt_s, dkt_s, dvt_s, dr_s,
+def load_kernel(wq_ref, wk_ref, wv_ref, wo_ref, q_out, k_out, v_out, o_out, sems):
+    pairs = ((wq_ref, q_out), (wk_ref, k_out), (wv_ref, v_out), (wo_ref, o_out))
+    copies = [
+        pltpu.make_async_copy(source, target, sems.at[i])
+        for i, (source, target) in enumerate(pairs)
+    ]
+    for copy in copies:
+        copy.start()
+    for copy in copies:
+        copy.wait()
+
+
+def load_weights(*weights):
+    return pl.pallas_call(
+        load_kernel,
+        out_shape=tuple(jax.ShapeDtypeStruct(w.shape, w.dtype) for w in weights),
+        in_specs=[HBM] * 4,
+        out_specs=(VMEM,) * 4,
+        scratch_shapes=[pltpu.SemaphoreType.DMA((4,))],
+        compiler_params=WIDE,
+    )(*weights)
+
+
+def score_bias(last):
+    row = lax.broadcasted_iota(jnp.int32, (N, N), 0) >= 2 * QUAD
+    col = lax.broadcasted_iota(jnp.int32, (N, N), 1) >= 2 * QUAD
+    return jnp.where(jnp.logical_and(row != col, last == 1), F32(-1e30), F32(0.0))
+
+
+def softmax_t(kh, qth, bias):
+    s = dot(kh, qth) * FACTOR + bias
+    e = jnp.exp(s - jnp.max(s, axis=0, keepdims=True))
+    return e * (1.0 / jnp.sum(e, axis=0, keepdims=True))
+
+
+def forward_kernel(
+    last_ref, tok_ref, cot_ref, lon_ref, lat_ref, diag_ref, wq_ref, wk_ref, wv_ref,
+    g_ref, q_ref, k_ref, v_ref, c_ref,
+    x_s, c_s, ot_s,
 ):
     for i in range(HALF):
         x_s[HALF * i : HALF * (i + 1), :] = tok_ref[HALF + i].astype(F32)[HALF:]
@@ -47,30 +87,56 @@
     q = dot(x, wq_ref[...]).astype(BF16)
     k = dot(x, wk_ref[...]).astype(BF16)
     v = dot(x, wv_ref[...]).astype(BF16)
-    dot_t = dot(wo_ref[...], c, NT).astype(BF16)
     qt = q.T
-    kt = k.T
     vt = v.T
-    factor = 1.0 / math.sqrt(DH)
-    row = lax.broadcasted_iota(jnp.int32, (N, N), 0) >= 2 * QUAD
-    col = lax.broadcasted_iota(jnp.int32, (N, N), 1) >= 2 * QUAD
-    bias = jnp.where(jnp.logical_and(row != col, last_ref[0] == 1), F32(-1e30), F32(0.0))
+    bias = score_bias(last_ref[0])
     for h in range(HEADS):
         at = slice(DH * h, DH * (h + 1))
-        kh, vh = k[:, at], v[:, at]
-        qth, kth, vth, doth = qt[at], kt[at], vt[at], dot_t[at]
-        s = dot(kh, qth) * factor + bias
-        e = jnp.exp(s - jnp.max(s, axis=0, keepdims=True))
-        p = e * (1.0 / jnp.sum(e, axis=0, keepdims=True))
-        pb = p.astype(BF16)
-        ot_s[at, :] = dot(vth, pb).astype(BF16)
-        dp = dot(vh, doth)
-        dvt_s[at, :] = dot(doth, pb, NT).astype(BF16)
+        pb = softmax_t(k[:, at], qt[at], bias).astype(BF16)
+        ot_s[at, :] = dot(vt[at], pb).astype(BF16)
+    g_ref[...] = dot(ot_s[...], c).astype(BF16)
+    q_ref[...] = q
+    k_ref[...] = k
+    v_ref[...] = v
+    c_ref[...] = c
+
+
+def forward_call(last, tokens, cotangent, lon, lat, diag, wq, wk, wv):
+    flat = jax.ShapeDtypeStruct((N, D), BF16)
+    return pl.pallas_call(
+        forward_kernel,
+        out_shape=(jax.ShapeDtypeStruct((D, D), BF16), flat, flat, flat, flat),
+        in_specs=[SMEM] + [VMEM] * 8,
+        out_specs=(VMEM,) * 5,
+        scratch_shapes=[
+            pltpu.VMEM((N, D), F32),
+            pltpu.VMEM((N, D), F32),
+            pltpu.VMEM((D, N), BF16),
+        ],
+        compiler_params=PARAMS,
+    )(last, tokens, cotangent, lon, lat, diag, wq, wk, wv)
+
+
+def backward_kernel(
+    last_ref, q_ref, k_ref, v_ref, c_ref, wq_ref, wk_ref, wv_ref, wo_ref,
+    own_out, lon_out, lat_out, diag_out,
+    dqt_s, dkt_s, dvt_s, dr_s,
+):
+    k = k_ref[...]
+    v = v_ref[...]
+    qt = q_ref[...].T
+    kt = k.T
+    dot_t = dot(wo_ref[...], c_ref[...], NT).astype(BF16)
+    bias = score_bias(last_ref[0])
+    for h in range(HEADS):
+        at = slice(DH * h, DH * (h + 1))
+        p = softmax_t(k[:, at], qt[at], bias)
+        dp = dot(v[:, at], dot_t[at])
+        dvt_s[at, :] = dot(dot_t[at], p.astype(BF16), NT).astype(BF16)
         inner = jnp.sum(p * dp, axis=0, keepdims=True)
-        ds = (factor * p * (dp - inner)).astype(BF16)
-        dqt_s[at, :] = dot(kth, ds).astype(BF16)
-        dkt_s[at, :] = dot(qth, ds, NT).astype(BF16)
-    g_ref[...] = dot(ot_s[...], c).astype(BF16)
+        ds = (FACTOR * p * (dp - inner)).astype(BF16)
+        dqt_s[at, :] = dot(kt[at], ds).astype(BF16)
+        dkt_s[at, :] = dot(qt[at], ds, NT).astype(BF16)
     dr_s[...] = (
         dot(dqt_s[...].T, wq_ref[...], NT)
         + dot(dkt_s[...].T, wk_ref[...], NT)
@@ -82,27 +148,25 @@
             ref[i] = dr_s[at : at + HALF, :].astype(BF16)
 
 
-def window_call(last, tokens, cotangent, lon, lat, diag, wq, wk, wv, wo):
+def backward_call(last, q, k, v, c, wq, wk, wv, wo):
     quad = jax.ShapeDtypeStruct((HALF, HALF, D), BF16)
     return pl.pallas_call(
-        window_kernel,
-        out_shape=(jax.ShapeDtypeStruct((D, D), BF16), quad, quad, quad, quad),
-        in_specs=[SMEM] + [VMEM] * 9,
-        out_specs=(VMEM,) * 5,
+        backward_kernel,
+        out_shape=(quad, quad, quad, quad),
+        in_specs=[SMEM] + [VMEM] * 8,
+        out_specs=(VMEM,) * 4,
         scratch_shapes=[
-            pltpu.VMEM((N, D), F32),
-            pltpu.VMEM((N, D), F32),
-            pltpu.VMEM((D, N), BF16),
             pltpu.VMEM((D, N), BF16),
             pltpu.VMEM((D, N), BF16),
             pltpu.VMEM((D, N), BF16),
             pltpu.VMEM((N, D), F32),
         ],
         compiler_params=PARAMS,
-    )(last, tokens, cotangent, lon, lat, diag, wq, wk, wv, wo)
-
-
-def sum_kernel(in_ref, out_ref):
+    )(last, q, k, v, c, wq, wk, wv, wo)
+
+
+def sum_kernel(in_ref, *rest):
+    out_ref = rest[-1]
     total = in_ref[0].astype(F32)
     for i in range(1, in_ref.shape[0]):
         total = total + in_ref[i].astype(F32)
@@ -111,14 +175,14 @@
         out_ref[i] = total
 
 
-def sum_and_repeat(parts, copies):
+def sum_and_repeat(parts, copies, *after):
     return pl.pallas_call(
         sum_kernel,
         out_shape=jax.ShapeDtypeStruct((copies,) + parts.shape[1:], BF16),
-        in_specs=[VMEM],
+        in_specs=[VMEM] + [ANY] * len(after),
         out_specs=VMEM,
         compiler_params=PARAMS,
-    )(parts)
+    )(parts, *after)
 
 
 def finish_kernel(g_ref, own_ref, lon_ref, lat_ref, diag_ref, dtok_ref, dout_ref):
@@ -162,18 +226,19 @@
     lon = shifted(jnp.stack([tokens[HALF:, :HALF], cotangent[HALF:, :HALF]]), 0, -1)
     diag = shifted(jnp.stack([tokens[:HALF, :HALF], cotangent[:HALF, :HALF]]), -1, -1)
     last = (lax.axis_index(LAT) == lax.axis_size(LAT) - 1).astype(jnp.int32).reshape(1)
-    g, own, lon, lat, diag = window_call(
-        last, tokens, cotangent, lon, lat, diag, w_query, w_key, w_value, w_output
-    )
-    lat = shifted(lat, 1, 0)
-    lon = shifted(lon, 0, 1)
-    diag = shifted(diag, 1, 1)
+    wq, wk, wv, wo = load_weights(w_query, w_key, w_value, w_output)
+    g, q, k, v, c = forward_call(last, tokens, cotangent, lon, lat, diag, wq, wk, wv)
     n_plane = lax.axis_size(PLANE)
     n_z = lax.axis_size("z")
     parts = g.reshape(n_plane, D // n_plane, D)
     parts = lax.all_to_all(parts, PLANE, 0, 0, tiled=True)
-    parts = lax.all_to_all(sum_and_repeat(parts, n_z), "z", 0, 0, tiled=True)
-    parts = lax.all_to_all(sum_and_repeat(parts, n_plane), PLANE, 0, 0, tiled=True)
+    own, lon, lat, diag = backward_call(last, q, k, v, c, wq, wk, wv, wo)
+    parts = lax.all_to_all(sum_and_repeat(parts, n_z, own), "z", 0, 0, tiled=True)
+    lat = shifted(lat, 1, 0)
+    lon = shifted(lon, 0, 1)
+    diag = shifted(diag, 1, 1)
+    parts = sum_and_repeat(parts, n_plane, lon, lat, diag)
+    parts = lax.all_to_all(parts, PLANE, 0, 0, tiled=True)
     return finish_call(parts.reshape(D, D), own, lon, lat, diag)
 
 

time: 105 us -> 94 us (0.90)
  blocking collectives: 39 us -> 20.1 us
  waiting for transfers between devices: 7.34 us -> 11.8 us
  Pallas kernels: 10.5 us -> 14.2 us
  local copies, waits for them, and re-layouts: 4.25 us -> 1.07 us
  starting transfers between devices: 42.9 us -> 45.3 us
    all_to_all x1 -> x0, blocking collectives: 19.8 us -> none  [per_device(): parts = lax.all_to_all(sum_and_repeat(parts, n_z), 'z', 0, 0, tiled=True)]
    all_to_all x1 -> x2, waiting for transfers between devices: 0.01 us -> 5.96 us  [the longest x1 5.96 us: per_device(): parts = lax.all_to_all(parts, PLANE, 0, 0, tiled=True)]
    all_to_all x1 -> x2, starting transfers between devices: 8.91 us -> 13.3 us  [the longest x1 7.1 us: per_device(): parts = lax.all_to_all(parts, PLANE, 0, 0, tiled=True)]
    pallas_call x1 -> x3, Pallas kernels: 8.07 us -> 11.9 us  [the longest x1 5.58 us: backward_call(): pl.pallas_call(backward_kernel, out_shape=(quad, quad, quad, quad), in_sp...]
    unnamed x12 -> x6, local copies, waits for them, and re-layouts: 3.14 us -> 0.02 us
    ppermute x6, starting transfers between devices: 33.9 us -> 32.1 us  [shifted(): return lax.ppermute(value, axes, pairs)]
    ppermute x6, waiting for transfers between devices: 7.34 us -> 5.85 us  [shifted(): return lax.ppermute(value, axes, pairs)]
  transfers between devices with their start and end apart: 7 -> 8, of which waited for: 3 -> 3; matrix products, arithmetic and copies ran while one was open for 0% -> 0% of each run, Pallas kernels for 0% -> 9%
where the time goes in v2:
time: 94 us; the launch traced here: 93.5 us
  starting transfers between devices  45.3 us (48%)
  blocking collectives  20.1 us (21%)
  Pallas kernels  14.2 us (15%)
  waiting for transfers between devices  11.8 us (13%)
  local copies, waits for them, and re-layouts  1.07 us (1%)
    ppermute x6, starting transfers between devices, shifted(): return lax.ppermute(value, axes, pairs)  32.1 us
    all_to_all x1, blocking collectives, per_device(): parts = lax.all_to_all(parts, PLANE, 0, 0, tiled=True)  20.1 us
    all_to_all x1, starting transfers between devices, per_device(): parts = lax.all_to_all(parts, PLANE, 0, 0, tiled=True)  7.1 us
    all_to_all x1, starting transfers between devices, per_device(): lax.all_to_all(sum_and_repeat(parts, n_z, own), 'z', 0, 0, tiled=True)  6.18 us
    all_to_all x1, waiting for transfers between devices, per_device(): parts = lax.all_to_all(parts, PLANE, 0, 0, tiled=True)  5.96 us
    ppermute x6, waiting for transfers between devices, shifted(): return lax.ppermute(value, axes, pairs)  5.85 us
    pallas_call x1, Pallas kernels, backward_call(): pl.pallas_call(backward_kernel, out_shape=(quad, quad, quad, quad), in_sp...  5.58 us
    pallas_call x1, Pallas kernels, forward_call(): pl.pallas_call(forward_kernel, out_shape=(jax.ShapeDtypeStruct((D, D), BF...  3.91 us
  transfers between devices with their start and end apart: 8, of which 3 were waited for; matrix products, arithmetic and copies ran while one was open for 0% of the time, Pallas kernels for 9%

profile of v2, /device:TPU:1, one launch (start us, length us, event | category | flops | bytes accessed | tf_op | source)
XLA Modules:
  0.0 93.5 jit_solution(11830817200849472493)
XLA Ops:
  0.6 1.1 %slice_bitcast_fusion = (bf16[1,6,6,512]{3,2,1,0:T(8,128)(2,1)S(1)}, bf16[1,6,6,512]{3,2,1,0:T(8,128)(2,1)S(1)}, bf16[1,6,6,512]{3,2,1,0:T(8,128)(2,1)S(1)}, bf1...) fusion(bf16[12,12,512]{2,1,0:T(8,128)(2,1)} %cot_ref.1, ...), kind=kLoop, calls=%fused_computation.3 | loop fusion | bytes 442368 | tf_op jit(solution)/shard_map/stack | solution.py:227
  1.7 8.8 %collective-permute-start = (bf16[2,6,6,512]{3,2,1,0:T(8,128)(2,1)S(1)}, bf16[2,6,6,512]{3,2,1,0:T(8,128)(2,1)S(1)}, u32[]{:S(2)}, u32[]{:S(2)}) collective-permute-start(bf16[2,6,6,512]{3,2,1,0:T(8,128)(2,1)S(1)} %pad_maximum_fusion), channel_id=1, source_target_pairs={{0,63},{1,0},{2,1},{3,2},{4,3},{5,4},{6,5},{7,6},{8,7},{9,8},{10,9... | collective-permute-start | bytes 221192 | tf_op jit(solution)/shard_map/ppermute | solution.py:221
  10.5 1.9 %collective-permute-start.1 = (bf16[2,6,6,512]{3,2,1,0:T(8,128)(2,1)S(1)}, bf16[2,6,6,512]{3,2,1,0:T(8,128)(2,1)S(1)}, u32[]{:S(2)}, u32[]{:S(2)}) collective-permute-start(bf16[2,6,6,512]{3,2,1,0:T(8,128)(2,1)S(1)} %pad_maximum_fusion.1), channel_id=1, source_target_pairs={{0,448},{64,0},{128,64},{192,128},{256,192},{320,256},{384,320},{4... | collective-permute-start | bytes 221192 | tf_op jit(solution)/shard_map/ppermute | solution.py:221
  12.5 12.0 %collective-permute-start.2 = (bf16[2,6,6,512]{3,2,1,0:T(8,128)(2,1)S(1)}, bf16[2,6,6,512]{3,2,1,0:T(8,128)(2,1)S(1)}, u32[]{:S(2)}, u32[]{:S(2)}) collective-permute-start(bf16[2,6,6,512]{3,2,1,0:T(8,128)(2,1)S(1)} %pad_maximum_fusion.2), channel_id=1, source_target_pairs={{0,511},{1,448},{2,449},{3,450},{4,451},{5,452},{6,453},{7,454},{8... | collective-permute-start | bytes 221192 | tf_op jit(solution)/shard_map/ppermute | solution.py:221
  24.5 0.0 copy-start
  24.5 0.0 copy-start.1
  24.5 2.4 %shard_map.77 = (bf16[512,512]{1,0:T(8,128)(2,1)S(1)}, bf16[512,512]{1,0:T(8,128)(2,1)S(1)}, bf16[512,512]{1,0:T(8,128)(2,1)S(1)}, bf16[512,512]{1,0:T(8,128)(2,1)}) custom-call(bf16[512,512]{1,0:T(8,128)(2,1)} %wq_ref.1, bf16[512,512]{1,0:T(8,128)(2,1)} %wk_ref.1, bf16[512,512]{1,0:T(8,128)(2,1)} %wv_ref.1, bf16[512,512]{1,0:T(8,128)(2,1)} %wo_ref.1), custom_call_target="tpu_custom_call" | custom-call | tf_op jit(solution)/shard_map/pallas_call | solution.py:51
  26.9 0.0 collective-permute-done.lon_ref
  26.9 0.0 collective-permute-done.1.lat_ref
  26.9 0.0 collective-permute-done.2.diag_ref
  26.9 0.0 copy-done
  27.0 0.0 copy-done.1
  27.0 3.9 %shard_map.78 = (bf16[512,512]{1,0:T(8,128)(2,1)}, bf16[144,512]{1,0:T(8,128)(2,1)S(1)}, bf16[144,512]{1,0:T(8,128)(2,1)S(1)}, bf16[144,512]{1,0:T(8,128)(2,1)S(1)}, bf16[144,512]{1,0:T(8,128)(2,1)S(1)}) custom-call(s32[1]{0:T(128)} %bitcast.last_ref, bf16[12,12,512]{2,1,0:T(8,128)(2,1)S(1)} %copy-done, bf16[12,12,512]{2,1,0:T(8,128)(2,1)S(1)} %copy-done.1, ...), custom_call_target="tpu_custom_call" | custom-call | tf_op jit(solution)/shard_map/pallas_call | solution.py:106
  30.9 0.0 copy-start.2
  30.9 7.1 %all-to-all-start = ((bf16[32,16,512]{2,1,0:T(8,128)(2,1)}), bf16[32,16,512]{2,1,0:T(8,128)(2,1)S(1)}, u32[]{:S(2)}, u32[]{:S(2)}) async-start(bf16[32,16,512]{2,1,0:T(8,128)(2,1)} %bitcast.7), calls=%async_computation | async-start | bytes 1048576 | tf_op jit(solution)/shard_map/all_to_all | solution.py:234
  38.0 0.0 copy-done.2
  38.0 5.6 %shard_map.79 = (bf16[6,6,512]{2,1,0:T(8,128)(2,1)S(1)}, bf16[6,6,512]{2,1,0:T(8,128)(2,1)S(1)}, bf16[6,6,512]{2,1,0:T(8,128)(2,1)S(1)}, bf16[6,6,512]{2,1,0:T(8,128)(2,1)S(1)}) custom-call(s32[1]{0:T(128)} %bitcast.last_ref, bf16[144,512]{1,0:T(8,128)(2,1)S(1)} %get-tuple-element.19.q_ref, bf16[144,512]{1,0:T(8,128)(2,1)S(1)} %get-tuple-element.20.k_ref, ...), custom_call_target="tpu_custom_call" | custom-call | tf_op jit(solution)/shard_map/pallas_call | solution.py:153
  43.6 6.0 %all-to-all-done.in_ref = bf16[32,16,512]{2,1,0:T(8,128)(2,1)S(1)} async-done(((bf16[32,16,512]{2,1,0:T(8,128)(2,1)}), bf16[32,16,512]{2,1,0:T(8,128)(2,1)S(1)}, u32[]{:S(2)}, u32[]{:S(2)}) %all-to-all-start) | async-done | bytes 524320 | tf_op jit(solution)/shard_map/all_to_all | solution.py:234
  49.5 0.8 shard_map.80
  50.3 6.2 %all-to-all-start.1 = ((bf16[16,16,512]{2,1,0:T(8,128)(2,1)}), bf16[16,16,512]{2,1,0:T(8,128)(2,1)S(1)}, u32[]{:S(2)}, u32[]{:S(2)}) async-start(bf16[16,16,512]{2,1,0:T(8,128)(2,1)} %shard_map.80), calls=%async_computation.1 | async-start | bytes 524288 | tf_op jit(solution)/shard_map/all_to_all | solution.py:236
  56.5 2.8 %collective-permute-start.3 = (bf16[6,6,512]{2,1,0:T(8,128)(2,1)S(1)}, bf16[6,6,512]{2,1,0:T(8,128)(2,1)S(1)}, u32[]{:S(2)}, u32[]{:S(2)}) collective-permute-start(bf16[6,6,512]{2,1,0:T(8,128)(2,1)S(1)} %get-tuple-element.25), channel_id=1, source_target_pairs={{0,1},{1,2},{2,3},{3,4},{4,5},{5,6},{6,7},{7,8},{8,9},{9,10},{10,1... | collective-permute-start | bytes 110600 | tf_op jit(solution)/shard_map/ppermute | solution.py:221
  59.3 3.2 %collective-permute-start.4 = (bf16[6,6,512]{2,1,0:T(8,128)(2,1)S(1)}, bf16[6,6,512]{2,1,0:T(8,128)(2,1)S(1)}, u32[]{:S(2)}, u32[]{:S(2)}) collective-permute-start(bf16[6,6,512]{2,1,0:T(8,128)(2,1)S(1)} %get-tuple-element.26), channel_id=1, source_target_pairs={{0,64},{64,128},{128,192},{192,256},{256,320},{320,384},{384,448},... | collective-permute-start | bytes 110600 | tf_op jit(solution)/shard_map/ppermute | solution.py:221
  62.5 3.5 %collective-permute-start.5 = (bf16[6,6,512]{2,1,0:T(8,128)(2,1)S(1)}, bf16[6,6,512]{2,1,0:T(8,128)(2,1)S(1)}, u32[]{:S(2)}, u32[]{:S(2)}) collective-permute-start(bf16[6,6,512]{2,1,0:T(8,128)(2,1)S(1)} %get-tuple-element.27), channel_id=1, source_target_pairs={{0,65},{1,66},{2,67},{3,68},{4,69},{5,70},{6,71},{7,72},{8,73},{9,... | collective-permute-start | bytes 110600 | tf_op jit(solution)/shard_map/ppermute | solution.py:221
  65.9 0.0 collective-permute-done.3.rest_0_.lon_ref
  65.9 2.3 %collective-permute-done.4.rest_1_.lat_ref = bf16[6,6,512]{2,1,0:T(8,128)(2,1)S(1)} collective-permute-done((bf16[6,6,512]{2,1,0:T(8,128)(2,1)S(1)}, bf16[6,6,512]{2,1,0:T(8,128)(2,1)S(1)}, u32[]{:S(2)}, u32[]{:S(2)}) %collective-permute-start.4) | collective-permute-done | bytes 36896 | tf_op jit(solution)/shard_map/ppermute | solution.py:221
  68.2 3.5 %collective-permute-done.5.rest_2_.diag_ref = bf16[6,6,512]{2,1,0:T(8,128)(2,1)S(1)} collective-permute-done((bf16[6,6,512]{2,1,0:T(8,128)(2,1)S(1)}, bf16[6,6,512]{2,1,0:T(8,128)(2,1)S(1)}, u32[]{:S(2)}, u32[]{:S(2)}) %collective-permute-start.5) | collective-permute-done | bytes 36896 | tf_op jit(solution)/shard_map/ppermute | solution.py:221
  71.8 0.0 all-to-all-done.1.in_ref
  71.8 0.1 shard_map.81
  71.9 20.1 %all_to_all.15 = bf16[32,16,512]{2,1,0:T(8,128)(2,1)S(1)} all-to-all(bf16[32,16,512]{2,1,0:T(8,128)(2,1)S(1)} %shard_map.81), channel_id=1, replica_groups=mesh['y'=4,'xh'=2,'z'=16,'xl'=2,'core'=2] {'y','xh','xl','core'}, dimensions={0} | all-to-all | bytes 1048576 | tf_op jit(solution)/shard_map/all_to_all | solution.py:241
  92.0 1.4 %shard_map.82 = (bf16[12,12,512]{2,1,0:T(8,128)(2,1)}, f32[512,512]{1,0:T(8,128)}) custom-call(bf16[512,512]{1,0:T(8,128)(2,1)S(1)} %bitcast.15, bf16[6,6,512]{2,1,0:T(8,128)(2,1)S(1)} %get-tuple-element.24.rest_0_.own_ref, bf16[6,6,512]{2,1,0:T(8,128)(2,1)S(1)} %collective-permute-done.3.rest_0_.lon_ref, ...), custom_call_target="tpu_custom_call" | custom-call | tf_op jit(solution)/shard_map/pallas_call | solution.py:200
  (3 shorter events, 0.1 us)
Async XLA Ops:
  1.7 25.2 %collective-permute-start = (bf16[2,6,6,512]{3,2,1,0:T(8,128)(2,1)S(1)}, bf16[2,6,6,512]{3,2,1,0:T(8,128)(2,1)S(1)}, u32[]{:S(2)}, u32[]{:S(2)}) collective-permute-start(bf16[2,6,6,512]{3,2,1,0:T(8,128)(2,1)S(1)} %pad_maximum_fusion), channel_id=1, source_target_pairs={{0,63},{1,0},{2,1},{3,2},{4,3},{5,4},{6,5},{7,6},{8,7},{9,8},{10,9... | collective-permute-start | bytes 221192 | tf_op jit(solution)/shard_map/ppermute | solution.py:221
  10.5 16.4 %collective-permute-start.1 = (bf16[2,6,6,512]{3,2,1,0:T(8,128)(2,1)S(1)}, bf16[2,6,6,512]{3,2,1,0:T(8,128)(2,1)S(1)}, u32[]{:S(2)}, u32[]{:S(2)}) collective-permute-start(bf16[2,6,6,512]{3,2,1,0:T(8,128)(2,1)S(1)} %pad_maximum_fusion.1), channel_id=1, source_target_pairs={{0,448},{64,0},{128,64},{192,128},{256,192},{320,256},{384,320},{4... | collective-permute-start | bytes 221192 | tf_op jit(solution)/shard_map/ppermute | solution.py:221
  12.5 14.4 %collective-permute-start.2 = (bf16[2,6,6,512]{3,2,1,0:T(8,128)(2,1)S(1)}, bf16[2,6,6,512]{3,2,1,0:T(8,128)(2,1)S(1)}, u32[]{:S(2)}, u32[]{:S(2)}) collective-permute-start(bf16[2,6,6,512]{3,2,1,0:T(8,128)(2,1)S(1)} %pad_maximum_fusion.2), channel_id=1, source_target_pairs={{0,511},{1,448},{2,449},{3,450},{4,451},{5,452},{6,453},{7,454},{8... | collective-permute-start | bytes 221192 | tf_op jit(solution)/shard_map/ppermute | solution.py:221
  24.5 2.5 %copy-start = (bf16[12,12,512]{2,1,0:T(8,128)(2,1)S(1)}, bf16[12,12,512]{2,1,0:T(8,128)(2,1)}, u32[]{:S(2)}) copy-start(bf16[12,12,512]{2,1,0:T(8,128)(2,1)} %tok_ref.1) | copy-start | bytes 442372
  24.5 2.5 %copy-start.1 = (bf16[12,12,512]{2,1,0:T(8,128)(2,1)S(1)}, bf16[12,12,512]{2,1,0:T(8,128)(2,1)}, u32[]{:S(2)}) copy-start(bf16[12,12,512]{2,1,0:T(8,128)(2,1)} %cot_ref.1) | copy-start | bytes 442372
  30.9 7.1 %copy-start.2 = (bf16[512,512]{1,0:T(8,128)(2,1)S(1)}, bf16[512,512]{1,0:T(8,128)(2,1)}, u32[]{:S(2)}) copy-start(bf16[512,512]{1,0:T(8,128)(2,1)} %get-tuple-element.23.wo_ref) | copy-start | bytes 1572868
  30.9 18.7 %all-to-all-start = ((bf16[32,16,512]{2,1,0:T(8,128)(2,1)}), bf16[32,16,512]{2,1,0:T(8,128)(2,1)S(1)}, u32[]{:S(2)}, u32[]{:S(2)}) async-start(bf16[32,16,512]{2,1,0:T(8,128)(2,1)} %bitcast.7), calls=%async_computation | async-start | bytes 1048576 | tf_op jit(solution)/shard_map/all_to_all | solution.py:234
  50.3 21.5 %all-to-all-start.1 = ((bf16[16,16,512]{2,1,0:T(8,128)(2,1)}), bf16[16,16,512]{2,1,0:T(8,128)(2,1)S(1)}, u32[]{:S(2)}, u32[]{:S(2)}) async-start(bf16[16,16,512]{2,1,0:T(8,128)(2,1)} %shard_map.80), calls=%async_computation.1 | async-start | bytes 524288 | tf_op jit(solution)/shard_map/all_to_all | solution.py:236
  56.5 9.4 %collective-permute-start.3 = (bf16[6,6,512]{2,1,0:T(8,128)(2,1)S(1)}, bf16[6,6,512]{2,1,0:T(8,128)(2,1)S(1)}, u32[]{:S(2)}, u32[]{:S(2)}) collective-permute-start(bf16[6,6,512]{2,1,0:T(8,128)(2,1)S(1)} %get-tuple-element.25), channel_id=1, source_target_pairs={{0,1},{1,2},{2,3},{3,4},{4,5},{5,6},{6,7},{7,8},{8,9},{9,10},{10,1... | collective-permute-start | bytes 110600 | tf_op jit(solution)/shard_map/ppermute | solution.py:221
  59.3 8.9 %collective-permute-start.4 = (bf16[6,6,512]{2,1,0:T(8,128)(2,1)S(1)}, bf16[6,6,512]{2,1,0:T(8,128)(2,1)S(1)}, u32[]{:S(2)}, u32[]{:S(2)}) collective-permute-start(bf16[6,6,512]{2,1,0:T(8,128)(2,1)S(1)} %get-tuple-element.26), channel_id=1, source_target_pairs={{0,64},{64,128},{128,192},{192,256},{256,320},{320,384},{384,448},... | collective-permute-start | bytes 110600 | tf_op jit(solution)/shard_map/ppermute | solution.py:221
  62.5 9.3 %collective-permute-start.5 = (bf16[6,6,512]{2,1,0:T(8,128)(2,1)S(1)}, bf16[6,6,512]{2,1,0:T(8,128)(2,1)S(1)}, u32[]{:S(2)}, u32[]{:S(2)}) collective-permute-start(bf16[6,6,512]{2,1,0:T(8,128)(2,1)S(1)} %get-tuple-element.27), channel_id=1, source_target_pairs={{0,65},{1,66},{2,67},{3,68},{4,69},{5,70},{6,71},{7,72},{8,73},{9,... | collective-permute-start | bytes 110600 | tf_op jit(solution)/shard_map/ppermute | solution.py:221

commit v3 on v2

--- a/solution.py
+++ b/solution.py
@@ -64,10 +64,23 @@
     return jnp.where(jnp.logical_and(row != col, last == 1), F32(-1e30), F32(0.0))
 
 
-def softmax_t(kh, qth, bias):
-    s = dot(kh, qth) * FACTOR + bias
-    e = jnp.exp(s - jnp.max(s, axis=0, keepdims=True))
+def softmax_t(scores, bias):
+    s = scores * (FACTOR * math.log2(math.e)) + bias
+    e = jnp.exp2(s - jnp.max(s, axis=0, keepdims=True))
     return e * (1.0 / jnp.sum(e, axis=0, keepdims=True))
+
+
+def staggered(depth, before, between, after):
+    rows = [slice(DH * h, DH * (h + 1)) for h in range(HEADS)]
+    ready = {h: before(rows[h]) for h in range(depth)}
+    done = {}
+    for h in range(HEADS + depth):
+        if h + depth < HEADS:
+            ready[h + depth] = before(rows[h + depth])
+        if h >= depth:
+            after(rows[h - depth], done.pop(h - depth))
+        if h < HEADS:
+            done[h] = between(ready.pop(h))
 
 
 def forward_kernel(
@@ -90,10 +103,17 @@
     qt = q.T
     vt = v.T
     bias = score_bias(last_ref[0])
-    for h in range(HEADS):
-        at = slice(DH * h, DH * (h + 1))
-        pb = softmax_t(k[:, at], qt[at], bias).astype(BF16)
+
+    def before(at):
+        return dot(k[:, at], qt[at])
+
+    def between(scores):
+        return softmax_t(scores, bias).astype(BF16)
+
+    def after(at, pb):
         ot_s[at, :] = dot(vt[at], pb).astype(BF16)
+
+    staggered(3, before, between, after)
     g_ref[...] = dot(ot_s[...], c).astype(BF16)
     q_ref[...] = q
     k_ref[...] = k
@@ -128,15 +148,23 @@
     kt = k.T
     dot_t = dot(wo_ref[...], c_ref[...], NT).astype(BF16)
     bias = score_bias(last_ref[0])
-    for h in range(HEADS):
-        at = slice(DH * h, DH * (h + 1))
-        p = softmax_t(k[:, at], qt[at], bias)
-        dp = dot(v[:, at], dot_t[at])
-        dvt_s[at, :] = dot(dot_t[at], p.astype(BF16), NT).astype(BF16)
+
+    def before(at):
+        return dot(k[:, at], qt[at]), dot(v[:, at], dot_t[at])
+
+    def between(products):
+        scores, dp = products
+        p = softmax_t(scores, bias)
         inner = jnp.sum(p * dp, axis=0, keepdims=True)
-        ds = (FACTOR * p * (dp - inner)).astype(BF16)
+        return p.astype(BF16), (FACTOR * p * (dp - inner)).astype(BF16)
+
+    def after(at, factors):
+        pb, ds = factors
+        dvt_s[at, :] = dot(dot_t[at], pb, NT).astype(BF16)
         dqt_s[at, :] = dot(kt[at], ds).astype(BF16)
         dkt_s[at, :] = dot(qt[at], ds, NT).astype(BF16)
+
+    staggered(2, before, between, after)
     dr_s[...] = (
         dot(dqt_s[...].T, wq_ref[...], NT)
         + dot(dkt_s[...].T, wk_ref[...], NT)
@@ -237,8 +265,9 @@
     lat = shifted(lat, 1, 0)
     lon = shifted(lon, 0, 1)
     diag = shifted(diag, 1, 1)
-    parts = sum_and_repeat(parts, n_plane, lon, lat, diag)
-    parts = lax.all_to_all(parts, PLANE, 0, 0, tiled=True)
+    parts = sum_and_repeat(parts, n_plane // 2, lon, lat, diag)
+    parts = lax.all_to_all(parts, ("y", "xh", "xl"), 0, 0, tiled=True)
+    parts = lax.all_gather(parts.reshape(n_plane // 2, 1, D // n_plane, D), "core", axis=1, tiled=True)
     return finish_call(parts.reshape(D, D), own, lon, lat, diag)
 
 

time: 94 us -> 91.4 us (0.972)
  Pallas kernels: 14.2 us -> 9.78 us
  waiting for transfers between devices: 11.8 us -> 14.7 us
  blocking collectives: 20.1 us -> 19 us
    all_to_all x1, blocking collectives: 20.1 us -> 12.4 us  [per_device(): parts = lax.all_to_all(parts, ('y', 'xh', 'xl'), 0, 0, tiled=True)]
    all_gather x0 -> x1, blocking collectives: none -> 6.6 us  [per_device(): lax.all_gather(parts.reshape(n_plane // 2, 1, D // n_plane, D), 'core', a...]
    all_to_all x1, waiting for transfers between devices: 5.96 us -> 8.83 us  [per_device(): parts = lax.all_to_all(parts, PLANE, 0, 0, tiled=True)]
    pallas_call x1, Pallas kernels: 5.58 us -> 2.7 us  [backward_call(): pl.pallas_call(backward_kernel, out_shape=(quad, quad, quad, quad), in_sp...]
    pallas_call x1, Pallas kernels: 3.91 us -> 2.41 us  [forward_call(): pl.pallas_call(forward_kernel, out_shape=(jax.ShapeDtypeStruct((D, D), BF...]
  transfers between devices with their start and end apart: 8 -> 8, of which waited for: 3 -> 3; matrix products, arithmetic and copies ran while one was open for 0% -> 0% of each run, Pallas kernels for 9% -> 6%
where the time goes in v3:
time: 91.4 us; the launch traced here: 90.8 us
  starting transfers between devices  45.4 us (50%)
  blocking collectives  19 us (21%)
  waiting for transfers between devices  14.7 us (16%)
  Pallas kernels  9.78 us (11%)
  local copies, waits for them, and re-layouts  1.07 us (1%)
    ppermute x6, starting transfers between devices, shifted(): return lax.ppermute(value, axes, pairs)  32.1 us
    all_to_all x1, blocking collectives, per_device(): parts = lax.all_to_all(parts, ('y', 'xh', 'xl'), 0, 0, tiled=True)  12.4 us
    all_to_all x1, waiting for transfers between devices, per_device(): parts = lax.all_to_all(parts, PLANE, 0, 0, tiled=True)  8.83 us
    all_to_all x1, starting transfers between devices, per_device(): parts = lax.all_to_all(parts, PLANE, 0, 0, tiled=True)  7.1 us
    all_gather x1, blocking collectives, per_device(): lax.all_gather(parts.reshape(n_plane // 2, 1, D // n_plane, D), 'core', a...  6.6 us
    all_to_all x1, starting transfers between devices, per_device(): lax.all_to_all(sum_and_repeat(parts, n_z, own), 'z', 0, 0, tiled=True)  6.18 us
    ppermute x6, waiting for transfers between devices, shifted(): return lax.ppermute(value, axes, pairs)  5.85 us
    pallas_call x1, Pallas kernels, backward_call(): pl.pallas_call(backward_kernel, out_shape=(quad, quad, quad, quad), in_sp...  2.7 us
  transfers between devices with their start and end apart: 8, of which 3 were waited for; matrix products, arithmetic and copies ran while one was open for 0% of the time, Pallas kernels for 6%

profile of v3, /device:TPU:1, one launch (start us, length us, event | category | flops | bytes accessed | tf_op | source)
XLA Modules:
  0.0 90.8 jit_solution(2458561703025764096)
XLA Ops:
  0.6 1.1 %slice_bitcast_fusion = (bf16[1,6,6,512]{3,2,1,0:T(8,128)(2,1)S(1)}, bf16[1,6,6,512]{3,2,1,0:T(8,128)(2,1)S(1)}, bf16[1,6,6,512]{3,2,1,0:T(8,128)(2,1)S(1)}, bf1...) fusion(bf16[12,12,512]{2,1,0:T(8,128)(2,1)} %cot_ref.1, ...), kind=kLoop, calls=%fused_computation.3 | loop fusion | bytes 442368 | tf_op jit(solution)/shard_map/stack | solution.py:255
  1.7 8.8 %collective-permute-start = (bf16[2,6,6,512]{3,2,1,0:T(8,128)(2,1)S(1)}, bf16[2,6,6,512]{3,2,1,0:T(8,128)(2,1)S(1)}, u32[]{:S(2)}, u32[]{:S(2)}) collective-permute-start(bf16[2,6,6,512]{3,2,1,0:T(8,128)(2,1)S(1)} %pad_maximum_fusion), channel_id=1, source_target_pairs={{0,63},{1,0},{2,1},{3,2},{4,3},{5,4},{6,5},{7,6},{8,7},{9,8},{10,9... | collective-permute-start | bytes 221192 | tf_op jit(solution)/shard_map/ppermute | solution.py:249
  10.5 1.9 %collective-permute-start.1 = (bf16[2,6,6,512]{3,2,1,0:T(8,128)(2,1)S(1)}, bf16[2,6,6,512]{3,2,1,0:T(8,128)(2,1)S(1)}, u32[]{:S(2)}, u32[]{:S(2)}) collective-permute-start(bf16[2,6,6,512]{3,2,1,0:T(8,128)(2,1)S(1)} %pad_maximum_fusion.1), channel_id=1, source_target_pairs={{0,448},{64,0},{128,64},{192,128},{256,192},{320,256},{384,320},{4... | collective-permute-start | bytes 221192 | tf_op jit(solution)/shard_map/ppermute | solution.py:249
  12.5 12.0 %collective-permute-start.2 = (bf16[2,6,6,512]{3,2,1,0:T(8,128)(2,1)S(1)}, bf16[2,6,6,512]{3,2,1,0:T(8,128)(2,1)S(1)}, u32[]{:S(2)}, u32[]{:S(2)}) collective-permute-start(bf16[2,6,6,512]{3,2,1,0:T(8,128)(2,1)S(1)} %pad_maximum_fusion.2), channel_id=1, source_target_pairs={{0,511},{1,448},{2,449},{3,450},{4,451},{5,452},{6,453},{7,454},{8... | collective-permute-start | bytes 221192 | tf_op jit(solution)/shard_map/ppermute | solution.py:249
  24.5 0.0 copy-start
  24.5 0.0 copy-start.1
  24.5 2.4 %shard_map.77 = (bf16[512,512]{1,0:T(8,128)(2,1)S(1)}, bf16[512,512]{1,0:T(8,128)(2,1)S(1)}, bf16[512,512]{1,0:T(8,128)(2,1)S(1)}, bf16[512,512]{1,0:T(8,128)(2,1)}) custom-call(bf16[512,512]{1,0:T(8,128)(2,1)} %wq_ref.1, bf16[512,512]{1,0:T(8,128)(2,1)} %wk_ref.1, bf16[512,512]{1,0:T(8,128)(2,1)} %wv_ref.1, bf16[512,512]{1,0:T(8,128)(2,1)} %wo_ref.1), custom_call_target="tpu_custom_call" | custom-call | tf_op jit(solution)/shard_map/pallas_call | solution.py:51
  26.9 0.0 collective-permute-done.lon_ref
  26.9 0.0 collective-permute-done.1.lat_ref
  26.9 0.0 collective-permute-done.2.diag_ref
  26.9 0.0 copy-done
  27.0 0.0 copy-done.1
  27.0 2.4 %shard_map.78 = (bf16[512,512]{1,0:T(8,128)(2,1)}, bf16[144,512]{1,0:T(8,128)(2,1)S(1)}, bf16[144,512]{1,0:T(8,128)(2,1)S(1)}, bf16[144,512]{1,0:T(8,128)(2,1)S(1)}, bf16[144,512]{1,0:T(8,128)(2,1)S(1)}) custom-call(s32[1]{0:T(128)} %bitcast.last_ref, bf16[12,12,512]{2,1,0:T(8,128)(2,1)S(1)} %copy-done, bf16[12,12,512]{2,1,0:T(8,128)(2,1)S(1)} %copy-done.1, ...), custom_call_target="tpu_custom_call" | custom-call | tf_op jit(solution)/shard_map/pallas_call | solution.py:126
  29.4 0.0 copy-start.2
  29.4 7.1 %all-to-all-start = ((bf16[32,16,512]{2,1,0:T(8,128)(2,1)}), bf16[32,16,512]{2,1,0:T(8,128)(2,1)S(1)}, u32[]{:S(2)}, u32[]{:S(2)}) async-start(bf16[32,16,512]{2,1,0:T(8,128)(2,1)} %bitcast.7), calls=%async_computation | async-start | bytes 1048576 | tf_op jit(solution)/shard_map/all_to_all | solution.py:262
  36.5 0.0 copy-done.2
  36.5 2.7 %shard_map.79 = (bf16[6,6,512]{2,1,0:T(8,128)(2,1)S(1)}, bf16[6,6,512]{2,1,0:T(8,128)(2,1)S(1)}, bf16[6,6,512]{2,1,0:T(8,128)(2,1)S(1)}, bf16[6,6,512]{2,1,0:T(8,128)(2,1)S(1)}) custom-call(s32[1]{0:T(128)} %bitcast.last_ref, bf16[144,512]{1,0:T(8,128)(2,1)S(1)} %get-tuple-element.19.q_ref, bf16[144,512]{1,0:T(8,128)(2,1)S(1)} %get-tuple-element.20.k_ref, ...), custom_call_target="tpu_custom_call" | custom-call | tf_op jit(solution)/shard_map/pallas_call | solution.py:181
  39.2 8.8 %all-to-all-done.in_ref = bf16[32,16,512]{2,1,0:T(8,128)(2,1)S(1)} async-done(((bf16[32,16,512]{2,1,0:T(8,128)(2,1)}), bf16[32,16,512]{2,1,0:T(8,128)(2,1)S(1)}, u32[]{:S(2)}, u32[]{:S(2)}) %all-to-all-start) | async-done | bytes 524320 | tf_op jit(solution)/shard_map/all_to_all | solution.py:262
  48.0 0.8 shard_map.80
  48.8 6.2 %all-to-all-start.1 = ((bf16[16,16,512]{2,1,0:T(8,128)(2,1)}), bf16[16,16,512]{2,1,0:T(8,128)(2,1)S(1)}, u32[]{:S(2)}, u32[]{:S(2)}) async-start(bf16[16,16,512]{2,1,0:T(8,128)(2,1)} %shard_map.80), calls=%async_computation.1 | async-start | bytes 524288 | tf_op jit(solution)/shard_map/all_to_all | solution.py:264
  55.0 2.8 %collective-permute-start.3 = (bf16[6,6,512]{2,1,0:T(8,128)(2,1)S(1)}, bf16[6,6,512]{2,1,0:T(8,128)(2,1)S(1)}, u32[]{:S(2)}, u32[]{:S(2)}) collective-permute-start(bf16[6,6,512]{2,1,0:T(8,128)(2,1)S(1)} %get-tuple-element.25), channel_id=1, source_target_pairs={{0,1},{1,2},{2,3},{3,4},{4,5},{5,6},{6,7},{7,8},{8,9},{9,10},{10,1... | collective-permute-start | bytes 110600 | tf_op jit(solution)/shard_map/ppermute | solution.py:249
  57.8 3.2 %collective-permute-start.4 = (bf16[6,6,512]{2,1,0:T(8,128)(2,1)S(1)}, bf16[6,6,512]{2,1,0:T(8,128)(2,1)S(1)}, u32[]{:S(2)}, u32[]{:S(2)}) collective-permute-start(bf16[6,6,512]{2,1,0:T(8,128)(2,1)S(1)} %get-tuple-element.26), channel_id=1, source_target_pairs={{0,64},{64,128},{128,192},{192,256},{256,320},{320,384},{384,448},... | collective-permute-start | bytes 110600 | tf_op jit(solution)/shard_map/ppermute | solution.py:249
  61.0 3.5 %collective-permute-start.5 = (bf16[6,6,512]{2,1,0:T(8,128)(2,1)S(1)}, bf16[6,6,512]{2,1,0:T(8,128)(2,1)S(1)}, u32[]{:S(2)}, u32[]{:S(2)}) collective-permute-start(bf16[6,6,512]{2,1,0:T(8,128)(2,1)S(1)} %get-tuple-element.27), channel_id=1, source_target_pairs={{0,65},{1,66},{2,67},{3,68},{4,69},{5,70},{6,71},{7,72},{8,73},{9,... | collective-permute-start | bytes 110600 | tf_op jit(solution)/shard_map/ppermute | solution.py:249
  64.4 0.0 collective-permute-done.3.rest_0_.lon_ref
  64.4 2.3 %collective-permute-done.4.rest_1_.lat_ref = bf16[6,6,512]{2,1,0:T(8,128)(2,1)S(1)} collective-permute-done((bf16[6,6,512]{2,1,0:T(8,128)(2,1)S(1)}, bf16[6,6,512]{2,1,0:T(8,128)(2,1)S(1)}, u32[]{:S(2)}, u32[]{:S(2)}) %collective-permute-start.4) | collective-permute-done | bytes 36896 | tf_op jit(solution)/shard_map/ppermute | solution.py:249
  66.7 3.5 %collective-permute-done.5.rest_2_.diag_ref = bf16[6,6,512]{2,1,0:T(8,128)(2,1)S(1)} collective-permute-done((bf16[6,6,512]{2,1,0:T(8,128)(2,1)S(1)}, bf16[6,6,512]{2,1,0:T(8,128)(2,1)S(1)}, u32[]{:S(2)}, u32[]{:S(2)}) %collective-permute-start.5) | collective-permute-done | bytes 36896 | tf_op jit(solution)/shard_map/ppermute | solution.py:249
  70.3 0.0 all-to-all-done.1.in_ref
  70.3 12.4 %all_to_all.15 = bf16[16,16,512]{2,1,0:T(8,128)(2,1)S(1)} all-to-all(bf16[16,16,512]{2,1,0:T(8,128)(2,1)S(1)} %shard_map.81), channel_id=1, replica_groups=mesh['y'=4,'xh'=2,'z'=16,'xl'=2,'core'=2] {'y','xh','xl'}, dimensions={0} | all-to-all | bytes 524288 | tf_op jit(solution)/shard_map/all_to_all | solution.py:269
  82.8 6.6 %all-gather = bf16[16,32,512]{2,1,0:T(8,128)(2,1)S(1)} all-gather(bf16[16,16,512]{2,1,0:T(8,128)(2,1)S(1)} %all_to_all.15), channel_id=2, replica_groups=mesh['y'=4,'xh'=2,'z'=16,'xl'=2,'core'=2] {'core'}, dimensions={1}, use_global_device_ids=true | all-gather | bytes 786432 | tf_op jit(solution)/shard_map/all_gather | solution.py:270
  89.4 1.4 %shard_map.82 = (bf16[12,12,512]{2,1,0:T(8,128)(2,1)}, f32[512,512]{1,0:T(8,128)}) custom-call(bf16[512,512]{1,0:T(8,128)(2,1)S(1)} %bitcast.15, bf16[6,6,512]{2,1,0:T(8,128)(2,1)S(1)} %get-tuple-element.24.rest_0_.own_ref, bf16[6,6,512]{2,1,0:T(8,128)(2,1)S(1)} %collective-permute-done.3.rest_0_.lon_ref, ...), custom_call_target="tpu_custom_call" | custom-call | tf_op jit(solution)/shard_map/pallas_call | solution.py:228
  (4 shorter events, 0.1 us)
Async XLA Ops:
  1.7 25.2 %collective-permute-start = (bf16[2,6,6,512]{3,2,1,0:T(8,128)(2,1)S(1)}, bf16[2,6,6,512]{3,2,1,0:T(8,128)(2,1)S(1)}, u32[]{:S(2)}, u32[]{:S(2)}) collective-permute-start(bf16[2,6,6,512]{3,2,1,0:T(8,128)(2,1)S(1)} %pad_maximum_fusion), channel_id=1, source_target_pairs={{0,63},{1,0},{2,1},{3,2},{4,3},{5,4},{6,5},{7,6},{8,7},{9,8},{10,9... | collective-permute-start | bytes 221192 | tf_op jit(solution)/shard_map/ppermute | solution.py:249
  10.5 16.4 %collective-permute-start.1 = (bf16[2,6,6,512]{3,2,1,0:T(8,128)(2,1)S(1)}, bf16[2,6,6,512]{3,2,1,0:T(8,128)(2,1)S(1)}, u32[]{:S(2)}, u32[]{:S(2)}) collective-permute-start(bf16[2,6,6,512]{3,2,1,0:T(8,128)(2,1)S(1)} %pad_maximum_fusion.1), channel_id=1, source_target_pairs={{0,448},{64,0},{128,64},{192,128},{256,192},{320,256},{384,320},{4... | collective-permute-start | bytes 221192 | tf_op jit(solution)/shard_map/ppermute | solution.py:249
  12.5 14.4 %collective-permute-start.2 = (bf16[2,6,6,512]{3,2,1,0:T(8,128)(2,1)S(1)}, bf16[2,6,6,512]{3,2,1,0:T(8,128)(2,1)S(1)}, u32[]{:S(2)}, u32[]{:S(2)}) collective-permute-start(bf16[2,6,6,512]{3,2,1,0:T(8,128)(2,1)S(1)} %pad_maximum_fusion.2), channel_id=1, source_target_pairs={{0,511},{1,448},{2,449},{3,450},{4,451},{5,452},{6,453},{7,454},{8... | collective-permute-start | bytes 221192 | tf_op jit(solution)/shard_map/ppermute | solution.py:249
  24.5 2.5 %copy-start = (bf16[12,12,512]{2,1,0:T(8,128)(2,1)S(1)}, bf16[12,12,512]{2,1,0:T(8,128)(2,1)}, u32[]{:S(2)}) copy-start(bf16[12,12,512]{2,1,0:T(8,128)(2,1)} %tok_ref.1) | copy-start | bytes 442372
  24.5 2.5 %copy-start.1 = (bf16[12,12,512]{2,1,0:T(8,128)(2,1)S(1)}, bf16[12,12,512]{2,1,0:T(8,128)(2,1)}, u32[]{:S(2)}) copy-start(bf16[12,12,512]{2,1,0:T(8,128)(2,1)} %cot_ref.1) | copy-start | bytes 442372
  29.4 7.1 %copy-start.2 = (bf16[512,512]{1,0:T(8,128)(2,1)S(1)}, bf16[512,512]{1,0:T(8,128)(2,1)}, u32[]{:S(2)}) copy-start(bf16[512,512]{1,0:T(8,128)(2,1)} %get-tuple-element.23.wo_ref) | copy-start | bytes 1572868
  29.4 18.7 %all-to-all-start = ((bf16[32,16,512]{2,1,0:T(8,128)(2,1)}), bf16[32,16,512]{2,1,0:T(8,128)(2,1)S(1)}, u32[]{:S(2)}, u32[]{:S(2)}) async-start(bf16[32,16,512]{2,1,0:T(8,128)(2,1)} %bitcast.7), calls=%async_computation | async-start | bytes 1048576 | tf_op jit(solution)/shard_map/all_to_all | solution.py:262
  48.8 21.5 %all-to-all-start.1 = ((bf16[16,16,512]{2,1,0:T(8,128)(2,1)}), bf16[16,16,512]{2,1,0:T(8,128)(2,1)S(1)}, u32[]{:S(2)}, u32[]{:S(2)}) async-start(bf16[16,16,512]{2,1,0:T(8,128)(2,1)} %shard_map.80), calls=%async_computation.1 | async-start | bytes 524288 | tf_op jit(solution)/shard_map/all_to_all | solution.py:264
  55.0 9.4 %collective-permute-start.3 = (bf16[6,6,512]{2,1,0:T(8,128)(2,1)S(1)}, bf16[6,6,512]{2,1,0:T(8,128)(2,1)S(1)}, u32[]{:S(2)}, u32[]{:S(2)}) collective-permute-start(bf16[6,6,512]{2,1,0:T(8,128)(2,1)S(1)} %get-tuple-element.25), channel_id=1, source_target_pairs={{0,1},{1,2},{2,3},{3,4},{4,5},{5,6},{6,7},{7,8},{8,9},{9,10},{10,1... | collective-permute-start | bytes 110600 | tf_op jit(solution)/shard_map/ppermute | solution.py:249
  57.8 8.9 %collective-permute-start.4 = (bf16[6,6,512]{2,1,0:T(8,128)(2,1)S(1)}, bf16[6,6,512]{2,1,0:T(8,128)(2,1)S(1)}, u32[]{:S(2)}, u32[]{:S(2)}) collective-permute-start(bf16[6,6,512]{2,1,0:T(8,128)(2,1)S(1)} %get-tuple-element.26), channel_id=1, source_target_pairs={{0,64},{64,128},{128,192},{192,256},{256,320},{320,384},{384,448},... | collective-permute-start | bytes 110600 | tf_op jit(solution)/shard_map/ppermute | solution.py:249
  61.0 9.3 %collective-permute-start.5 = (bf16[6,6,512]{2,1,0:T(8,128)(2,1)S(1)}, bf16[6,6,512]{2,1,0:T(8,128)(2,1)S(1)}, u32[]{:S(2)}, u32[]{:S(2)}) collective-permute-start(bf16[6,6,512]{2,1,0:T(8,128)(2,1)S(1)} %get-tuple-element.27), channel_id=1, source_target_pairs={{0,65},{1,66},{2,67},{3,68},{4,69},{5,70},{6,71},{7,72},{8,73},{9,... | collective-permute-start | bytes 110600 | tf_op jit(solution)/shard_map/ppermute | solution.py:249

commit v4 on v3

--- a/solution.py
+++ b/solution.py
@@ -15,10 +15,16 @@
 FACTOR = 1.0 / math.sqrt(DH)
 QUAD = HALF * HALF
 N = 4 * QUAD
-SPLIT = ("y", "xh", "z", "xl", "core")
+SPLIT = ("y", "xh", "zh", "zl", "xl", "core")
 LAT = ("y", "xh")
-LON = ("z", "xl", "core")
-PLANE = ("y", "xh", "xl", "core")
+LON = ("zh", "zl", "xl", "core")
+CHIPS = ("y", "xh", "zl", "xl")
+BLOCK = CHIPS + ("core",)
+FAR_ORDER = [(4 + i) % 8 for i in range(8)]
+CHIP_ORDER = [(22 + i) % 32 for i in range(32)]
+BLOCK_ORDER = [2 * chip + core for chip in CHIP_ORDER for core in range(2)]
+ROWS = 16
+COLS = 512 // 2
 F32 = jnp.float32
 BF16 = jnp.bfloat16
 NT = (((1,), (1,)), ((), ()))
@@ -114,7 +120,9 @@
         ot_s[at, :] = dot(vt[at], pb).astype(BF16)
 
     staggered(3, before, between, after)
-    g_ref[...] = dot(ot_s[...], c).astype(BF16)
+    g = dot(ot_s[...], c).astype(BF16).reshape(D // ROWS, ROWS, D)
+    for j in range(D // COLS):
+        g_ref[j] = g[:, :, COLS * j : COLS * (j + 1)]
     q_ref[...] = q
     k_ref[...] = k
     v_ref[...] = v
@@ -125,7 +133,7 @@
     flat = jax.ShapeDtypeStruct((N, D), BF16)
     return pl.pallas_call(
         forward_kernel,
-        out_shape=(jax.ShapeDtypeStruct((D, D), BF16), flat, flat, flat, flat),
+        out_shape=(jax.ShapeDtypeStruct((D // COLS, D // ROWS, ROWS, COLS), BF16), flat, flat, flat, flat),
         in_specs=[SMEM] + [VMEM] * 8,
         out_specs=(VMEM,) * 5,
         scratch_shapes=[
@@ -139,7 +147,7 @@
 
 def backward_kernel(
     last_ref, q_ref, k_ref, v_ref, c_ref, wq_ref, wk_ref, wv_ref, wo_ref,
-    own_out, lon_out, lat_out, diag_out,
+    own_out, lat_out, side_out,
     dqt_s, dkt_s, dvt_s, dr_s,
 ):
     k = k_ref[...]
@@ -170,7 +178,7 @@
         + dot(dkt_s[...].T, wk_ref[...], NT)
         + dot(dvt_s[...].T, wv_ref[...], NT)
     )
-    for part, ref in enumerate((own_out, lon_out, lat_out, diag_out)):
+    for part, ref in enumerate((own_out, side_out.at[0], lat_out, side_out.at[1])):
         for i in range(HALF):
             at = QUAD * part + HALF * i
             ref[i] = dr_s[at : at + HALF, :].astype(BF16)
@@ -180,9 +188,9 @@
     quad = jax.ShapeDtypeStruct((HALF, HALF, D), BF16)
     return pl.pallas_call(
         backward_kernel,
-        out_shape=(quad, quad, quad, quad),
+        out_shape=(quad, quad, jax.ShapeDtypeStruct((2, HALF, HALF, D), BF16)),
         in_specs=[SMEM] + [VMEM] * 8,
-        out_specs=(VMEM,) * 4,
+        out_specs=(VMEM,) * 3,
         scratch_shapes=[
             pltpu.VMEM((D, N), BF16),
             pltpu.VMEM((D, N), BF16),
@@ -191,6 +199,25 @@
         ],
         compiler_params=PARAMS,
     )(last, q, k, v, c, wq, wk, wv, wo)
+
+
+def sum_and_join_kernel(in_ref, lat_ref, side_ref, out_ref, join_ref):
+    join_ref[0] = lat_ref[...]
+    join_ref[1] = side_ref[1]
+    sum_kernel(in_ref, out_ref)
+
+
+def sum_and_join(parts, copies, lat, side):
+    return pl.pallas_call(
+        sum_and_join_kernel,
+        out_shape=(
+            jax.ShapeDtypeStruct((copies,) + parts.shape[1:], BF16),
+            jax.ShapeDtypeStruct(side.shape, BF16),
+        ),
+        in_specs=[VMEM] * 3,
+        out_specs=(VMEM,) * 2,
+        compiler_params=PARAMS,
+    )(parts, lat, side)
 
 
 def sum_kernel(in_ref, *rest):
@@ -213,28 +240,31 @@
     )(parts, *after)
 
 
-def finish_kernel(g_ref, own_ref, lon_ref, lat_ref, diag_ref, dtok_ref, dout_ref):
-    g = g_ref[...].astype(F32)
-    norm = jnp.sqrt(jnp.sum(g * g, keepdims=True))
-    dout_ref[...] = g * jnp.minimum(F32(1.0), F32(D) / (norm + 1e-6))
+def finish_kernel(g_ref, own_ref, side_ref, above_ref, dtok_ref, dout_ref):
+    blocks = [g_ref[j].astype(F32).reshape(D, COLS) for j in range(D // COLS)]
+    squares = sum(block * block for block in blocks)
+    norm = jnp.sqrt(jnp.sum(squares, keepdims=True))
+    scale = jnp.minimum(F32(1.0), F32(D) / (norm + 1e-6))
+    for j, block in enumerate(blocks):
+        dout_ref[:, COLS * j : COLS * (j + 1)] = block * scale
     for i in range(HALF):
-        top = (diag_ref[i].astype(F32), lat_ref[i].astype(F32))
+        top = (above_ref[1, i].astype(F32), above_ref[0, i].astype(F32))
         dtok_ref[i] = jnp.concatenate(top, axis=0).astype(BF16)
-        bottom = (lon_ref[i].astype(F32), own_ref[i].astype(F32))
+        bottom = (side_ref[0, i].astype(F32), own_ref[i].astype(F32))
         dtok_ref[HALF + i] = jnp.concatenate(bottom, axis=0).astype(BF16)
 
 
-def finish_call(g, own, lon, lat, diag):
+def finish_call(g, own, side, above):
     return pl.pallas_call(
         finish_kernel,
         out_shape=(
             jax.ShapeDtypeStruct((2 * HALF, 2 * HALF, D), BF16),
             jax.ShapeDtypeStruct((D, D), F32),
         ),
-        in_specs=[VMEM] * 5,
+        in_specs=[VMEM] * 4,
         out_specs=(VMEM, VMEM),
         compiler_params=PARAMS,
-    )(g, own, lon, lat, diag)
+    )(g, own, side, above)
 
 
 def shifted(value, lat_step, lon_step):
@@ -256,23 +286,25 @@
     last = (lax.axis_index(LAT) == lax.axis_size(LAT) - 1).astype(jnp.int32).reshape(1)
     wq, wk, wv, wo = load_weights(w_query, w_key, w_value, w_output)
     g, q, k, v, c = forward_call(last, tokens, cotangent, lon, lat, diag, wq, wk, wv)
-    n_plane = lax.axis_size(PLANE)
-    n_z = lax.axis_size("z")
-    parts = g.reshape(n_plane, D // n_plane, D)
-    parts = lax.all_to_all(parts, PLANE, 0, 0, tiled=True)
-    own, lon, lat, diag = backward_call(last, q, k, v, c, wq, wk, wv, wo)
-    parts = lax.all_to_all(sum_and_repeat(parts, n_z, own), "z", 0, 0, tiled=True)
-    lat = shifted(lat, 1, 0)
-    lon = shifted(lon, 0, 1)
-    diag = shifted(diag, 1, 1)
-    parts = sum_and_repeat(parts, n_plane // 2, lon, lat, diag)
-    parts = lax.all_to_all(parts, ("y", "xh", "xl"), 0, 0, tiled=True)
-    parts = lax.all_gather(parts.reshape(n_plane // 2, 1, D // n_plane, D), "core", axis=1, tiled=True)
-    return finish_call(parts.reshape(D, D), own, lon, lat, diag)
+    n_chips = lax.axis_size(CHIPS)
+    n_far = lax.axis_size("zh")
+    parts = g.reshape(2 * n_chips, ROWS, COLS)
+    parts = lax.all_to_all(parts, BLOCK, 0, 0, tiled=True)
+    own, lat, side = backward_call(last, q, k, v, c, wq, wk, wv, wo)
+    side = shifted(side, 0, 1)
+    parts, above = sum_and_join(parts, n_far, lat, side)
+    parts = lax.all_to_all(parts, "zh", 0, 0, axis_index_groups=[FAR_ORDER], tiled=True)
+    above = shifted(above, 1, 0)
+    parts = sum_and_repeat(parts, n_chips)
+    parts = lax.all_to_all(parts, CHIPS, 0, 0, tiled=True)
+    parts = parts.reshape(n_chips, 1, ROWS, COLS)
+    parts = lax.all_gather(parts, "core", axis=1, tiled=True)
+    parts = parts.reshape(D // COLS, D // ROWS, ROWS, COLS)
+    return finish_call(parts, own, side, above)
 
 
 def solution(mesh):
-    fine = Mesh(mesh.devices.reshape(4, 2, 16, 2, 2), SPLIT)
+    fine = Mesh(mesh.devices.reshape(4, 2, 8, 2, 2, 2), SPLIT)
     tiles = P(LAT, LON, None)
     return jax.shard_map(
         per_device,

time: 91.4 us -> 83.9 us (0.918)
  waiting for transfers between devices: 14.7 us -> 10.1 us
  starting transfers between devices: 45.4 us -> 42.1 us
    ppermute x6 -> x5, waiting for transfers between devices: 5.85 us -> 1.7 us  [shifted(): return lax.ppermute(value, axes, pairs)]
    all_to_all x2, starting transfers between devices: 13.3 us -> 11.4 us  [the longest x1 7.5 us: per_device(): parts = lax.all_to_all(parts, BLOCK, 0, 0, tiled=True)]
    all_to_all x1, blocking collectives: 12.4 us -> 14.3 us  [per_device(): lax.all_to_all(parts, 'zh', 0, 0, axis_index_groups=[FAR_ORDER], tiled=True)]
    ppermute x6 -> x5, starting transfers between devices: 32.1 us -> 30.8 us  [shifted(): return lax.ppermute(value, axes, pairs)]
    all_gather x1, blocking collectives: 6.6 us -> 5.36 us  [per_device(): parts = lax.all_gather(parts, 'core', axis=1, tiled=True)]
    pallas_call x2 -> x3, Pallas kernels: 5.1 us -> 5.21 us  [the longest x1 2.7 us: backward_call(): pl.pallas_call(backward_kernel, out_shape=(quad, quad, jax.ShapeDtypeStru...]
  transfers between devices with their start and end apart: 8 -> 7, of which waited for: 3 -> 3; matrix products, arithmetic and copies ran while one was open for 0% -> 0% of each run, Pallas kernels for 6% -> 6%
where the time goes in v4:
time: 83.9 us; the launch traced here: 83.4 us
  starting transfers between devices  42.1 us (50%)
  blocking collectives  19.7 us (23%)
  waiting for transfers between devices  10.1 us (12%)
  Pallas kernels  9.64 us (11%)
  local copies, waits for them, and re-layouts  1.07 us (1%)
    ppermute x5, starting transfers between devices, shifted(): return lax.ppermute(value, axes, pairs)  30.8 us
    all_to_all x1, blocking collectives, per_device(): lax.all_to_all(parts, 'zh', 0, 0, axis_index_groups=[FAR_ORDER], tiled=True)  14.3 us
    all_to_all x1, starting transfers between devices, per_device(): parts = lax.all_to_all(parts, BLOCK, 0, 0, tiled=True)  7.5 us
    all_gather x1, blocking collectives, per_device(): parts = lax.all_gather(parts, 'core', axis=1, tiled=True)  5.36 us
    all_to_all x1, waiting for transfers between devices, per_device(): parts = lax.all_to_all(parts, BLOCK, 0, 0, tiled=True)  4.67 us
    all_to_all x1, starting transfers between devices, per_device(): parts = lax.all_to_all(parts, CHIPS, 0, 0, tiled=True)  3.87 us
    all_to_all x1, waiting for transfers between devices, per_device(): parts = lax.all_to_all(parts, CHIPS, 0, 0, tiled=True)  3.69 us
    pallas_call x1, Pallas kernels, backward_call(): pl.pallas_call(backward_kernel, out_shape=(quad, quad, jax.ShapeDtypeStru...  2.7 us
  transfers between devices with their start and end apart: 7, of which 3 were waited for; matrix products, arithmetic and copies ran while one was open for 0% of the time, Pallas kernels for 6%

profile of v4, /device:TPU:1, one launch (start us, length us, event | category | flops | bytes accessed | tf_op | source)
XLA Modules:
  0.0 83.4 jit_solution(3121272793471569754)
XLA Ops:
  0.6 1.1 %slice_bitcast_fusion = (bf16[1,6,6,512]{3,2,1,0:T(8,128)(2,1)S(1)}, bf16[1,6,6,512]{3,2,1,0:T(8,128)(2,1)S(1)}, bf16[1,6,6,512]{3,2,1,0:T(8,128)(2,1)S(1)}, bf1...) fusion(bf16[12,12,512]{2,1,0:T(8,128)(2,1)} %cot_ref.1, ...), kind=kLoop, calls=%fused_computation.3 | loop fusion | bytes 442368 | tf_op jit(solution)/shard_map/stack | solution.py:285
  1.7 8.8 %collective-permute-start = (bf16[2,6,6,512]{3,2,1,0:T(8,128)(2,1)S(1)}, bf16[2,6,6,512]{3,2,1,0:T(8,128)(2,1)S(1)}, u32[]{:S(2)}, u32[]{:S(2)}) collective-permute-start(bf16[2,6,6,512]{3,2,1,0:T(8,128)(2,1)S(1)} %pad_maximum_fusion), channel_id=1, source_target_pairs={{0,63},{1,0},{2,1},{3,2},{4,3},{5,4},{6,5},{7,6},{8,7},{9,8},{10,9... | collective-permute-start | bytes 221192 | tf_op jit(solution)/shard_map/ppermute | solution.py:279
  10.5 1.9 %collective-permute-start.1 = (bf16[2,6,6,512]{3,2,1,0:T(8,128)(2,1)S(1)}, bf16[2,6,6,512]{3,2,1,0:T(8,128)(2,1)S(1)}, u32[]{:S(2)}, u32[]{:S(2)}) collective-permute-start(bf16[2,6,6,512]{3,2,1,0:T(8,128)(2,1)S(1)} %pad_maximum_fusion.1), channel_id=1, source_target_pairs={{0,448},{64,0},{128,64},{192,128},{256,192},{320,256},{384,320},{4... | collective-permute-start | bytes 221192 | tf_op jit(solution)/shard_map/ppermute | solution.py:279
  12.5 12.0 %collective-permute-start.2 = (bf16[2,6,6,512]{3,2,1,0:T(8,128)(2,1)S(1)}, bf16[2,6,6,512]{3,2,1,0:T(8,128)(2,1)S(1)}, u32[]{:S(2)}, u32[]{:S(2)}) collective-permute-start(bf16[2,6,6,512]{3,2,1,0:T(8,128)(2,1)S(1)} %pad_maximum_fusion.2), channel_id=1, source_target_pairs={{0,511},{1,448},{2,449},{3,450},{4,451},{5,452},{6,453},{7,454},{8... | collective-permute-start | bytes 221192 | tf_op jit(solution)/shard_map/ppermute | solution.py:279
  24.5 0.0 copy-start
  24.5 0.0 copy-start.1
  24.5 2.4 %shard_map.77 = (bf16[512,512]{1,0:T(8,128)(2,1)S(1)}, bf16[512,512]{1,0:T(8,128)(2,1)S(1)}, bf16[512,512]{1,0:T(8,128)(2,1)S(1)}, bf16[512,512]{1,0:T(8,128)(2,1)}) custom-call(bf16[512,512]{1,0:T(8,128)(2,1)} %wq_ref.1, bf16[512,512]{1,0:T(8,128)(2,1)} %wk_ref.1, bf16[512,512]{1,0:T(8,128)(2,1)} %wv_ref.1, bf16[512,512]{1,0:T(8,128)(2,1)} %wo_ref.1), custom_call_target="tpu_custom_call" | custom-call | tf_op jit(solution)/shard_map/pallas_call | solution.py:57
  26.9 0.0 collective-permute-done.lon_ref
  26.9 0.0 collective-permute-done.1.lat_ref
  26.9 0.0 collective-permute-done.2.diag_ref
  26.9 0.0 copy-done
  27.0 0.0 copy-done.1
  27.0 2.4 %shard_map.78 = (bf16[2,32,16,256]{3,2,1,0:T(8,128)(2,1)}, bf16[144,512]{1,0:T(8,128)(2,1)S(1)}, bf16[144,512]{1,0:T(8,128)(2,1)S(1)}, bf16[144,512]{1,0:T(8,128)(2,1)S(1)}, bf16[144,512]{1,0:T(8,128)(2,1)S(1)}) custom-call(s32[1]{0:T(128)} %bitcast.last_ref, bf16[12,12,512]{2,1,0:T(8,128)(2,1)S(1)} %copy-done, bf16[12,12,512]{2,1,0:T(8,128)(2,1)S(1)} %copy-done.1, ...), custom_call_target="tpu_custom_call" | custom-call | tf_op jit(solution)/shard_map/pallas_call | solution.py:134
  29.4 0.0 copy-start.2
  29.4 7.5 %all-to-all-start = ((bf16[64,16,256]{2,1,0:T(8,128)(2,1)}), bf16[64,16,256]{2,1,0:T(8,128)(2,1)S(1)}, u32[]{:S(2)}, u32[]{:S(2)}) async-start(bf16[64,16,256]{2,1,0:T(8,128)(2,1)} %bitcast.7), calls=%async_computation | async-start | bytes 1048576 | tf_op jit(solution)/shard_map/all_to_all | solution.py:292
  36.9 0.0 copy-done.2
  36.9 2.7 %shard_map.79 = (bf16[6,6,512]{2,1,0:T(8,128)(2,1)S(1)}, bf16[6,6,512]{2,1,0:T(8,128)(2,1)S(1)}, bf16[2,6,6,512]{3,2,1,0:T(8,128)(2,1)S(1)}) custom-call(s32[1]{0:T(128)} %bitcast.last_ref, bf16[144,512]{1,0:T(8,128)(2,1)S(1)} %get-tuple-element.20.q_ref, bf16[144,512]{1,0:T(8,128)(2,1)S(1)} %get-tuple-element.21.k_ref, ...), custom_call_target="tpu_custom_call" | custom-call | tf_op jit(solution)/shard_map/pallas_call | solution.py:189
  39.6 3.5 %collective-permute-start.3 = (bf16[2,6,6,512]{3,2,1,0:T(8,128)(2,1)S(1)}, bf16[2,6,6,512]{3,2,1,0:T(8,128)(2,1)S(1)}, u32[]{:S(2)}, u32[]{:S(2)}) collective-permute-start(bf16[2,6,6,512]{3,2,1,0:T(8,128)(2,1)S(1)} %get-tuple-element.26), channel_id=1, source_target_pairs={{0,1},{1,2},{2,3},{3,4},{4,5},{5,6},{6,7},{7,8},{8,9},{9,10},{10,1... | collective-permute-start | bytes 221192 | tf_op jit(solution)/shard_map/ppermute | solution.py:279
  43.2 1.7 %collective-permute-done.3.side_ref = bf16[2,6,6,512]{3,2,1,0:T(8,128)(2,1)S(1)} collective-permute-done((bf16[2,6,6,512]{3,2,1,0:T(8,128)(2,1)S(1)}, bf16[2,6,6,512]{3,2,1,0:T(8,128)(2,1)S(1)}, u32[]{:S(2)}, u32[]{:S(2)}) %collective-permute-start.3) | collective-permute-done | bytes 73760 | tf_op jit(solution)/shard_map/ppermute | solution.py:279
  44.8 4.7 %all-to-all-done.in_ref = bf16[64,16,256]{2,1,0:T(8,128)(2,1)S(1)} async-done(((bf16[64,16,256]{2,1,0:T(8,128)(2,1)}), bf16[64,16,256]{2,1,0:T(8,128)(2,1)S(1)}, u32[]{:S(2)}, u32[]{:S(2)}) %all-to-all-start) | async-done | bytes 524320 | tf_op jit(solution)/shard_map/all_to_all | solution.py:292
  49.5 0.1 shard_map.80
  49.6 14.3 %all_to_all.15.in_ref = bf16[8,16,256]{2,1,0:T(8,128)(2,1)S(1)} all-to-all(bf16[8,16,256]{2,1,0:T(8,128)(2,1)S(1)} %get-tuple-element.27), channel_id=1, replica_groups={{32,40,48,56,0,8,16,24},{33,41,49,57,1,9,17,25},{34,42,50,58,2,10,18,26..., dimensions={0} | all-to-all | bytes 131072 | tf_op jit(solution)/shard_map/all_to_all | solution.py:296
  63.9 0.7 shard_map.81
  64.6 3.9 %all-to-all-start.2 = ((bf16[32,16,256]{2,1,0:T(8,128)(2,1)}), bf16[32,16,256]{2,1,0:T(8,128)(2,1)S(1)}, u32[]{:S(2)}, u32[]{:S(2)}) async-start(bf16[32,16,256]{2,1,0:T(8,128)(2,1)} %shard_map.81), calls=%async_computation.2 | async-start | bytes 524288 | tf_op jit(solution)/shard_map/all_to_all | solution.py:299
  68.5 4.6 %collective-permute-start.4 = (bf16[2,6,6,512]{3,2,1,0:T(8,128)(2,1)S(1)}, bf16[2,6,6,512]{3,2,1,0:T(8,128)(2,1)S(1)}, u32[]{:S(2)}, u32[]{:S(2)}) collective-permute-start(bf16[2,6,6,512]{3,2,1,0:T(8,128)(2,1)S(1)} %get-tuple-element.29), channel_id=1, source_target_pairs={{0,64},{64,128},{128,192},{192,256},{256,320},{320,384},{384,448},... | collective-permute-start | bytes 221192 | tf_op jit(solution)/shard_map/ppermute | solution.py:279
  73.1 3.7 %all-to-all-done.2 = bf16[32,16,256]{2,1,0:T(8,128)(2,1)S(1)} async-done(((bf16[32,16,256]{2,1,0:T(8,128)(2,1)}), bf16[32,16,256]{2,1,0:T(8,128)(2,1)S(1)}, u32[]{:S(2)}, u32[]{:S(2)}) %all-to-all-start.2) | async-done | bytes 262176 | tf_op jit(solution)/shard_map/all_to_all | solution.py:299
  76.8 5.4 %all-gather = bf16[32,32,256]{2,1,0:T(8,128)(2,1)S(1)} all-gather(bf16[32,16,256]{2,1,0:T(8,128)(2,1)S(1)} %all-to-all-done.2), channel_id=2, replica_groups=mesh['y'=4,'xh'=2,'zh'=8,'zl'=2,'xl'=2,'core'=2] {'core'}, dimensions={1}, use_global_device_ids=true | all-gather | bytes 786432 | tf_op jit(solution)/shard_map/all_gather | solution.py:301
  82.1 0.0 collective-permute-done.4.above_ref
  82.1 1.3 %shard_map.82 = (bf16[12,12,512]{2,1,0:T(8,128)(2,1)}, f32[512,512]{1,0:T(8,128)}) custom-call(bf16[2,32,16,256]{3,2,1,0:T(8,128)(2,1)S(1)} %bitcast.15, bf16[6,6,512]{2,1,0:T(8,128)(2,1)S(1)} %get-tuple-element.28.own_ref, bf16[2,6,6,512]{3,2,1,0:T(8,128)(2,1)S(1)} %collective-permute-done.3.side_ref, ...), custom_call_target="tpu_custom_call" | custom-call | tf_op jit(solution)/shard_map/pallas_call | solution.py:258
  (3 shorter events, 0.1 us)
Async XLA Ops:
  1.7 25.2 %collective-permute-start = (bf16[2,6,6,512]{3,2,1,0:T(8,128)(2,1)S(1)}, bf16[2,6,6,512]{3,2,1,0:T(8,128)(2,1)S(1)}, u32[]{:S(2)}, u32[]{:S(2)}) collective-permute-start(bf16[2,6,6,512]{3,2,1,0:T(8,128)(2,1)S(1)} %pad_maximum_fusion), channel_id=1, source_target_pairs={{0,63},{1,0},{2,1},{3,2},{4,3},{5,4},{6,5},{7,6},{8,7},{9,8},{10,9... | collective-permute-start | bytes 221192 | tf_op jit(solution)/shard_map/ppermute | solution.py:279
  10.5 16.4 %collective-permute-start.1 = (bf16[2,6,6,512]{3,2,1,0:T(8,128)(2,1)S(1)}, bf16[2,6,6,512]{3,2,1,0:T(8,128)(2,1)S(1)}, u32[]{:S(2)}, u32[]{:S(2)}) collective-permute-start(bf16[2,6,6,512]{3,2,1,0:T(8,128)(2,1)S(1)} %pad_maximum_fusion.1), channel_id=1, source_target_pairs={{0,448},{64,0},{128,64},{192,128},{256,192},{320,256},{384,320},{4... | collective-permute-start | bytes 221192 | tf_op jit(solution)/shard_map/ppermute | solution.py:279
  12.5 14.4 %collective-permute-start.2 = (bf16[2,6,6,512]{3,2,1,0:T(8,128)(2,1)S(1)}, bf16[2,6,6,512]{3,2,1,0:T(8,128)(2,1)S(1)}, u32[]{:S(2)}, u32[]{:S(2)}) collective-permute-start(bf16[2,6,6,512]{3,2,1,0:T(8,128)(2,1)S(1)} %pad_maximum_fusion.2), channel_id=1, source_target_pairs={{0,511},{1,448},{2,449},{3,450},{4,451},{5,452},{6,453},{7,454},{8... | collective-permute-start | bytes 221192 | tf_op jit(solution)/shard_map/ppermute | solution.py:279
  24.5 2.5 %copy-start = (bf16[12,12,512]{2,1,0:T(8,128)(2,1)S(1)}, bf16[12,12,512]{2,1,0:T(8,128)(2,1)}, u32[]{:S(2)}) copy-start(bf16[12,12,512]{2,1,0:T(8,128)(2,1)} %tok_ref.1) | copy-start | bytes 442372
  24.5 2.5 %copy-start.1 = (bf16[12,12,512]{2,1,0:T(8,128)(2,1)S(1)}, bf16[12,12,512]{2,1,0:T(8,128)(2,1)}, u32[]{:S(2)}) copy-start(bf16[12,12,512]{2,1,0:T(8,128)(2,1)} %cot_ref.1) | copy-start | bytes 442372
  29.4 7.5 %copy-start.2 = (bf16[512,512]{1,0:T(8,128)(2,1)S(1)}, bf16[512,512]{1,0:T(8,128)(2,1)}, u32[]{:S(2)}) copy-start(bf16[512,512]{1,0:T(8,128)(2,1)} %get-tuple-element.24.wo_ref) | copy-start | bytes 1572868
  29.4 20.1 %all-to-all-start = ((bf16[64,16,256]{2,1,0:T(8,128)(2,1)}), bf16[64,16,256]{2,1,0:T(8,128)(2,1)S(1)}, u32[]{:S(2)}, u32[]{:S(2)}) async-start(bf16[64,16,256]{2,1,0:T(8,128)(2,1)} %bitcast.7), calls=%async_computation | async-start | bytes 1048576 | tf_op jit(solution)/shard_map/all_to_all | solution.py:292
  39.6 5.2 %collective-permute-start.3 = (bf16[2,6,6,512]{3,2,1,0:T(8,128)(2,1)S(1)}, bf16[2,6,6,512]{3,2,1,0:T(8,128)(2,1)S(1)}, u32[]{:S(2)}, u32[]{:S(2)}) collective-permute-start(bf16[2,6,6,512]{3,2,1,0:T(8,128)(2,1)S(1)} %get-tuple-element.26), channel_id=1, source_target_pairs={{0,1},{1,2},{2,3},{3,4},{4,5},{5,6},{6,7},{7,8},{8,9},{9,10},{10,1... | collective-permute-start | bytes 221192 | tf_op jit(solution)/shard_map/ppermute | solution.py:279
  64.6 12.1 %all-to-all-start.2 = ((bf16[32,16,256]{2,1,0:T(8,128)(2,1)}), bf16[32,16,256]{2,1,0:T(8,128)(2,1)S(1)}, u32[]{:S(2)}, u32[]{:S(2)}) async-start(bf16[32,16,256]{2,1,0:T(8,128)(2,1)} %shard_map.81), calls=%async_computation.2 | async-start | bytes 524288 | tf_op jit(solution)/shard_map/all_to_all | solution.py:299
  68.5 13.6 %collective-permute-start.4 = (bf16[2,6,6,512]{3,2,1,0:T(8,128)(2,1)S(1)}, bf16[2,6,6,512]{3,2,1,0:T(8,128)(2,1)S(1)}, u32[]{:S(2)}, u32[]{:S(2)}) collective-permute-start(bf16[2,6,6,512]{3,2,1,0:T(8,128)(2,1)S(1)} %get-tuple-element.29), channel_id=1, source_target_pairs={{0,64},{64,128},{128,192},{192,256},{256,320},{320,384},{384,448},... | collective-permute-start | bytes 221192 | tf_op jit(solution)/shard_map/ppermute | solution.py:279

commit v5 on v4

--- a/solution.py
+++ b/solution.py
@@ -241,7 +241,12 @@
 
 
 def finish_kernel(g_ref, own_ref, side_ref, above_ref, dtok_ref, dout_ref):
-    blocks = [g_ref[j].astype(F32).reshape(D, COLS) for j in range(D // COLS)]
+    rows = D // ROWS
+    order = [(20 + p) % (2 * rows) for p in range(2 * rows)]
+    blocks = [
+        jnp.concatenate([g_ref[p].astype(F32) for p in order[rows * j : rows * (j + 1)]])
+        for j in range(D // COLS)
+    ]
     squares = sum(block * block for block in blocks)
     norm = jnp.sqrt(jnp.sum(squares, keepdims=True))
     scale = jnp.minimum(F32(1.0), F32(D) / (norm + 1e-6))
@@ -296,10 +301,10 @@
     parts = lax.all_to_all(parts, "zh", 0, 0, axis_index_groups=[FAR_ORDER], tiled=True)
     above = shifted(above, 1, 0)
     parts = sum_and_repeat(parts, n_chips)
-    parts = lax.all_to_all(parts, CHIPS, 0, 0, tiled=True)
+    parts = lax.all_to_all(parts, CHIPS, 0, 0, axis_index_groups=[CHIP_ORDER], tiled=True)
     parts = parts.reshape(n_chips, 1, ROWS, COLS)
     parts = lax.all_gather(parts, "core", axis=1, tiled=True)
-    parts = parts.reshape(D // COLS, D // ROWS, ROWS, COLS)
+    parts = parts.reshape(2 * n_chips, ROWS, COLS)
     return finish_call(parts, own, side, above)
 
 

time: 83.9 us -> 83.4 us (level)
  starting transfers between devices: 42.1 us -> 43.6 us
  waiting for transfers between devices: 10.1 us -> 8.88 us
  blocking collectives: 19.7 us -> 18.5 us
    all_to_all x1, starting transfers between devices: 3.87 us -> 7.71 us  [per_device(): lax.all_to_all(parts, CHIPS, 0, 0, axis_index_groups=[CHIP_ORDER], tiled=...]
    all_to_all x1, waiting for transfers between devices: 3.69 us -> 0.74 us  [per_device(): lax.all_to_all(parts, CHIPS, 0, 0, axis_index_groups=[CHIP_ORDER], tiled=...]
    ppermute x5, starting transfers between devices: 30.8 us -> 28.4 us  [shifted(): return lax.ppermute(value, axes, pairs)]
    ppermute x5, waiting for transfers between devices: 1.7 us -> 3.47 us  [shifted(): return lax.ppermute(value, axes, pairs)]
    all_gather x1, blocking collectives: 5.36 us -> 4.25 us  [per_device(): parts = lax.all_gather(parts, 'core', axis=1, tiled=True)]
  transfers between devices with their start and end apart: 7 -> 7, of which waited for: 3 -> 4; matrix products, arithmetic and copies ran while one was open for 0% -> 0% of each run, Pallas kernels for 6% -> 6%
where the time goes in v5:
time: 83.4 us; the launch traced here: 82.6 us
  starting transfers between devices  43.6 us (52%)
  blocking collectives  18.5 us (22%)
  Pallas kernels  9.64 us (12%)
  waiting for transfers between devices  8.88 us (11%)
  local copies, waits for them, and re-layouts  1.07 us (1%)
    ppermute x5, starting transfers between devices, shifted(): return lax.ppermute(value, axes, pairs)  28.4 us
    all_to_all x1, blocking collectives, per_device(): lax.all_to_all(parts, 'zh', 0, 0, axis_index_groups=[FAR_ORDER], tiled=True)  14.3 us
    all_to_all x1, starting transfers between devices, per_device(): lax.all_to_all(parts, CHIPS, 0, 0, axis_index_groups=[CHIP_ORDER], tiled=...  7.71 us
    all_to_all x1, starting transfers between devices, per_device(): parts = lax.all_to_all(parts, BLOCK, 0, 0, tiled=True)  7.5 us
    all_to_all x1, waiting for transfers between devices, per_device(): parts = lax.all_to_all(parts, BLOCK, 0, 0, tiled=True)  4.67 us
    all_gather x1, blocking collectives, per_device(): parts = lax.all_gather(parts, 'core', axis=1, tiled=True)  4.25 us
    ppermute x5, waiting for transfers between devices, shifted(): return lax.ppermute(value, axes, pairs)  3.47 us
    pallas_call x1, Pallas kernels, backward_call(): pl.pallas_call(backward_kernel, out_shape=(quad, quad, jax.ShapeDtypeStru...  2.7 us
  transfers between devices with their start and end apart: 7, of which 4 were waited for; matrix products, arithmetic and copies ran while one was open for 0% of the time, Pallas kernels for 6%

profile of v5, /device:TPU:1, one launch (start us, length us, event | category | flops | bytes accessed | tf_op | source)
XLA Modules:
  0.0 82.6 jit_solution(15044959738196077922)
XLA Ops:
  0.6 1.1 %slice_bitcast_fusion = (bf16[1,6,6,512]{3,2,1,0:T(8,128)(2,1)S(1)}, bf16[1,6,6,512]{3,2,1,0:T(8,128)(2,1)S(1)}, bf16[1,6,6,512]{3,2,1,0:T(8,128)(2,1)S(1)}, bf1...) fusion(bf16[12,12,512]{2,1,0:T(8,128)(2,1)} %cot_ref.1, ...), kind=kLoop, calls=%fused_computation.3 | loop fusion | bytes 442368 | tf_op jit(solution)/shard_map/stack | solution.py:290
  1.7 8.8 %collective-permute-start = (bf16[2,6,6,512]{3,2,1,0:T(8,128)(2,1)S(1)}, bf16[2,6,6,512]{3,2,1,0:T(8,128)(2,1)S(1)}, u32[]{:S(2)}, u32[]{:S(2)}) collective-permute-start(bf16[2,6,6,512]{3,2,1,0:T(8,128)(2,1)S(1)} %pad_maximum_fusion), channel_id=1, source_target_pairs={{0,63},{1,0},{2,1},{3,2},{4,3},{5,4},{6,5},{7,6},{8,7},{9,8},{10,9... | collective-permute-start | bytes 221192 | tf_op jit(solution)/shard_map/ppermute | solution.py:284
  10.5 1.9 %collective-permute-start.1 = (bf16[2,6,6,512]{3,2,1,0:T(8,128)(2,1)S(1)}, bf16[2,6,6,512]{3,2,1,0:T(8,128)(2,1)S(1)}, u32[]{:S(2)}, u32[]{:S(2)}) collective-permute-start(bf16[2,6,6,512]{3,2,1,0:T(8,128)(2,1)S(1)} %pad_maximum_fusion.1), channel_id=1, source_target_pairs={{0,448},{64,0},{128,64},{192,128},{256,192},{320,256},{384,320},{4... | collective-permute-start | bytes 221192 | tf_op jit(solution)/shard_map/ppermute | solution.py:284
  12.5 12.0 %collective-permute-start.2 = (bf16[2,6,6,512]{3,2,1,0:T(8,128)(2,1)S(1)}, bf16[2,6,6,512]{3,2,1,0:T(8,128)(2,1)S(1)}, u32[]{:S(2)}, u32[]{:S(2)}) collective-permute-start(bf16[2,6,6,512]{3,2,1,0:T(8,128)(2,1)S(1)} %pad_maximum_fusion.2), channel_id=1, source_target_pairs={{0,511},{1,448},{2,449},{3,450},{4,451},{5,452},{6,453},{7,454},{8... | collective-permute-start | bytes 221192 | tf_op jit(solution)/shard_map/ppermute | solution.py:284
  24.5 0.0 copy-start
  24.5 0.0 copy-start.1
  24.5 2.4 %shard_map.77 = (bf16[512,512]{1,0:T(8,128)(2,1)S(1)}, bf16[512,512]{1,0:T(8,128)(2,1)S(1)}, bf16[512,512]{1,0:T(8,128)(2,1)S(1)}, bf16[512,512]{1,0:T(8,128)(2,1)}) custom-call(bf16[512,512]{1,0:T(8,128)(2,1)} %wq_ref.1, bf16[512,512]{1,0:T(8,128)(2,1)} %wk_ref.1, bf16[512,512]{1,0:T(8,128)(2,1)} %wv_ref.1, bf16[512,512]{1,0:T(8,128)(2,1)} %wo_ref.1), custom_call_target="tpu_custom_call" | custom-call | tf_op jit(solution)/shard_map/pallas_call | solution.py:57
  26.9 0.0 collective-permute-done.lon_ref
  26.9 0.0 collective-permute-done.1.lat_ref
  26.9 0.0 collective-permute-done.2.diag_ref
  26.9 0.0 copy-done
  27.0 0.0 copy-done.1
  27.0 2.4 %shard_map.78 = (bf16[2,32,16,256]{3,2,1,0:T(8,128)(2,1)}, bf16[144,512]{1,0:T(8,128)(2,1)S(1)}, bf16[144,512]{1,0:T(8,128)(2,1)S(1)}, bf16[144,512]{1,0:T(8,128)(2,1)S(1)}, bf16[144,512]{1,0:T(8,128)(2,1)S(1)}) custom-call(s32[1]{0:T(128)} %bitcast.last_ref, bf16[12,12,512]{2,1,0:T(8,128)(2,1)S(1)} %copy-done, bf16[12,12,512]{2,1,0:T(8,128)(2,1)S(1)} %copy-done.1, ...), custom_call_target="tpu_custom_call" | custom-call | tf_op jit(solution)/shard_map/pallas_call | solution.py:134
  29.4 0.0 copy-start.2
  29.4 7.5 %all-to-all-start = ((bf16[64,16,256]{2,1,0:T(8,128)(2,1)}), bf16[64,16,256]{2,1,0:T(8,128)(2,1)S(1)}, u32[]{:S(2)}, u32[]{:S(2)}) async-start(bf16[64,16,256]{2,1,0:T(8,128)(2,1)} %bitcast.7), calls=%async_computation | async-start | bytes 1048576 | tf_op jit(solution)/shard_map/all_to_all | solution.py:297
  36.9 0.0 copy-done.2
  36.9 2.7 %shard_map.79 = (bf16[6,6,512]{2,1,0:T(8,128)(2,1)S(1)}, bf16[6,6,512]{2,1,0:T(8,128)(2,1)S(1)}, bf16[2,6,6,512]{3,2,1,0:T(8,128)(2,1)S(1)}) custom-call(s32[1]{0:T(128)} %bitcast.last_ref, bf16[144,512]{1,0:T(8,128)(2,1)S(1)} %get-tuple-element.20.q_ref, bf16[144,512]{1,0:T(8,128)(2,1)S(1)} %get-tuple-element.21.k_ref, ...), custom_call_target="tpu_custom_call" | custom-call | tf_op jit(solution)/shard_map/pallas_call | solution.py:189
  39.6 3.5 %collective-permute-start.3 = (bf16[2,6,6,512]{3,2,1,0:T(8,128)(2,1)S(1)}, bf16[2,6,6,512]{3,2,1,0:T(8,128)(2,1)S(1)}, u32[]{:S(2)}, u32[]{:S(2)}) collective-permute-start(bf16[2,6,6,512]{3,2,1,0:T(8,128)(2,1)S(1)} %get-tuple-element.26), channel_id=1, source_target_pairs={{0,1},{1,2},{2,3},{3,4},{4,5},{5,6},{6,7},{7,8},{8,9},{9,10},{10,1... | collective-permute-start | bytes 221192 | tf_op jit(solution)/shard_map/ppermute | solution.py:284
  43.2 1.7 %collective-permute-done.3.side_ref = bf16[2,6,6,512]{3,2,1,0:T(8,128)(2,1)S(1)} collective-permute-done((bf16[2,6,6,512]{3,2,1,0:T(8,128)(2,1)S(1)}, bf16[2,6,6,512]{3,2,1,0:T(8,128)(2,1)S(1)}, u32[]{:S(2)}, u32[]{:S(2)}) %collective-permute-start.3) | collective-permute-done | bytes 73760 | tf_op jit(solution)/shard_map/ppermute | solution.py:284
  44.8 4.7 %all-to-all-done.in_ref = bf16[64,16,256]{2,1,0:T(8,128)(2,1)S(1)} async-done(((bf16[64,16,256]{2,1,0:T(8,128)(2,1)}), bf16[64,16,256]{2,1,0:T(8,128)(2,1)S(1)}, u32[]{:S(2)}, u32[]{:S(2)}) %all-to-all-start) | async-done | bytes 524320 | tf_op jit(solution)/shard_map/all_to_all | solution.py:297
  49.5 0.1 shard_map.80
  49.6 14.3 %all_to_all.15.in_ref = bf16[8,16,256]{2,1,0:T(8,128)(2,1)S(1)} all-to-all(bf16[8,16,256]{2,1,0:T(8,128)(2,1)S(1)} %get-tuple-element.27), channel_id=1, replica_groups={{32,40,48,56,0,8,16,24},{33,41,49,57,1,9,17,25},{34,42,50,58,2,10,18,26..., dimensions={0} | all-to-all | bytes 131072 | tf_op jit(solution)/shard_map/all_to_all | solution.py:301
  63.9 0.7 shard_map.81
  64.6 7.7 %all-to-all-start.2 = ((bf16[32,16,256]{2,1,0:T(8,128)(2,1)}), bf16[32,16,256]{2,1,0:T(8,128)(2,1)S(1)}, u32[]{:S(2)}, u32[]{:S(2)}) async-start(bf16[32,16,256]{2,1,0:T(8,128)(2,1)} %shard_map.81), calls=%async_computation.2 | async-start | bytes 524288 | tf_op jit(solution)/shard_map/all_to_all | solution.py:304
  72.3 2.2 %collective-permute-start.4 = (bf16[2,6,6,512]{3,2,1,0:T(8,128)(2,1)S(1)}, bf16[2,6,6,512]{3,2,1,0:T(8,128)(2,1)S(1)}, u32[]{:S(2)}, u32[]{:S(2)}) collective-permute-start(bf16[2,6,6,512]{3,2,1,0:T(8,128)(2,1)S(1)} %get-tuple-element.29), channel_id=1, source_target_pairs={{0,64},{64,128},{128,192},{192,256},{256,320},{320,384},{384,448},... | collective-permute-start | bytes 221192 | tf_op jit(solution)/shard_map/ppermute | solution.py:284
  74.5 0.7 all-to-all-done.2
  75.3 4.3 %all-gather = bf16[32,32,256]{2,1,0:T(8,128)(2,1)S(1)} all-gather(bf16[32,16,256]{2,1,0:T(8,128)(2,1)S(1)} %all-to-all-done.2), channel_id=2, replica_groups=mesh['y'=4,'xh'=2,'zh'=8,'zl'=2,'xl'=2,'core'=2] {'core'}, dimensions={1}, use_global_device_ids=true | all-gather | bytes 786432 | tf_op jit(solution)/shard_map/all_gather | solution.py:306
  79.5 1.8 %collective-permute-done.4.above_ref = bf16[2,6,6,512]{3,2,1,0:T(8,128)(2,1)S(1)} collective-permute-done((bf16[2,6,6,512]{3,2,1,0:T(8,128)(2,1)S(1)}, bf16[2,6,6,512]{3,2,1,0:T(8,128)(2,1)S(1)}, u32[]{:S(2)}, u32[]{:S(2)}) %collective-permute-start.4) | collective-permute-done | bytes 73760 | tf_op jit(solution)/shard_map/ppermute | solution.py:284
  81.3 1.3 %shard_map.82 = (bf16[12,12,512]{2,1,0:T(8,128)(2,1)}, f32[512,512]{1,0:T(8,128)}) custom-call(bf16[64,16,256]{2,1,0:T(8,128)(2,1)S(1)} %bitcast.15, bf16[6,6,512]{2,1,0:T(8,128)(2,1)S(1)} %get-tuple-element.28.own_ref, bf16[2,6,6,512]{3,2,1,0:T(8,128)(2,1)S(1)} %collective-permute-done.3.side_ref, bf16[2,6,6,512]{3,2,1,0:T(8,128)(2,1)S(1)} %collective-permute-done.4.above_ref), custom_call_target="tpu_custom_call" | custom-call | tf_op jit(solution)/shard_map/pallas_call | solution.py:263
  (3 shorter events, 0.1 us)
Async XLA Ops:
  1.7 25.2 %collective-permute-start = (bf16[2,6,6,512]{3,2,1,0:T(8,128)(2,1)S(1)}, bf16[2,6,6,512]{3,2,1,0:T(8,128)(2,1)S(1)}, u32[]{:S(2)}, u32[]{:S(2)}) collective-permute-start(bf16[2,6,6,512]{3,2,1,0:T(8,128)(2,1)S(1)} %pad_maximum_fusion), channel_id=1, source_target_pairs={{0,63},{1,0},{2,1},{3,2},{4,3},{5,4},{6,5},{7,6},{8,7},{9,8},{10,9... | collective-permute-start | bytes 221192 | tf_op jit(solution)/shard_map/ppermute | solution.py:284
  10.5 16.4 %collective-permute-start.1 = (bf16[2,6,6,512]{3,2,1,0:T(8,128)(2,1)S(1)}, bf16[2,6,6,512]{3,2,1,0:T(8,128)(2,1)S(1)}, u32[]{:S(2)}, u32[]{:S(2)}) collective-permute-start(bf16[2,6,6,512]{3,2,1,0:T(8,128)(2,1)S(1)} %pad_maximum_fusion.1), channel_id=1, source_target_pairs={{0,448},{64,0},{128,64},{192,128},{256,192},{320,256},{384,320},{4... | collective-permute-start | bytes 221192 | tf_op jit(solution)/shard_map/ppermute | solution.py:284
  12.5 14.4 %collective-permute-start.2 = (bf16[2,6,6,512]{3,2,1,0:T(8,128)(2,1)S(1)}, bf16[2,6,6,512]{3,2,1,0:T(8,128)(2,1)S(1)}, u32[]{:S(2)}, u32[]{:S(2)}) collective-permute-start(bf16[2,6,6,512]{3,2,1,0:T(8,128)(2,1)S(1)} %pad_maximum_fusion.2), channel_id=1, source_target_pairs={{0,511},{1,448},{2,449},{3,450},{4,451},{5,452},{6,453},{7,454},{8... | collective-permute-start | bytes 221192 | tf_op jit(solution)/shard_map/ppermute | solution.py:284
  24.5 2.5 %copy-start = (bf16[12,12,512]{2,1,0:T(8,128)(2,1)S(1)}, bf16[12,12,512]{2,1,0:T(8,128)(2,1)}, u32[]{:S(2)}) copy-start(bf16[12,12,512]{2,1,0:T(8,128)(2,1)} %tok_ref.1) | copy-start | bytes 442372
  24.5 2.5 %copy-start.1 = (bf16[12,12,512]{2,1,0:T(8,128)(2,1)S(1)}, bf16[12,12,512]{2,1,0:T(8,128)(2,1)}, u32[]{:S(2)}) copy-start(bf16[12,12,512]{2,1,0:T(8,128)(2,1)} %cot_ref.1) | copy-start | bytes 442372
  29.4 7.5 %copy-start.2 = (bf16[512,512]{1,0:T(8,128)(2,1)S(1)}, bf16[512,512]{1,0:T(8,128)(2,1)}, u32[]{:S(2)}) copy-start(bf16[512,512]{1,0:T(8,128)(2,1)} %get-tuple-element.24.wo_ref) | copy-start | bytes 1572868
  29.4 20.1 %all-to-all-start = ((bf16[64,16,256]{2,1,0:T(8,128)(2,1)}), bf16[64,16,256]{2,1,0:T(8,128)(2,1)S(1)}, u32[]{:S(2)}, u32[]{:S(2)}) async-start(bf16[64,16,256]{2,1,0:T(8,128)(2,1)} %bitcast.7), calls=%async_computation | async-start | bytes 1048576 | tf_op jit(solution)/shard_map/all_to_all | solution.py:297
  39.6 5.2 %collective-permute-start.3 = (bf16[2,6,6,512]{3,2,1,0:T(8,128)(2,1)S(1)}, bf16[2,6,6,512]{3,2,1,0:T(8,128)(2,1)S(1)}, u32[]{:S(2)}, u32[]{:S(2)}) collective-permute-start(bf16[2,6,6,512]{3,2,1,0:T(8,128)(2,1)S(1)} %get-tuple-element.26), channel_id=1, source_target_pairs={{0,1},{1,2},{2,3},{3,4},{4,5},{5,6},{6,7},{7,8},{8,9},{9,10},{10,1... | collective-permute-start | bytes 221192 | tf_op jit(solution)/shard_map/ppermute | solution.py:284
  64.6 10.7 %all-to-all-start.2 = ((bf16[32,16,256]{2,1,0:T(8,128)(2,1)}), bf16[32,16,256]{2,1,0:T(8,128)(2,1)S(1)}, u32[]{:S(2)}, u32[]{:S(2)}) async-start(bf16[32,16,256]{2,1,0:T(8,128)(2,1)} %shard_map.81), calls=%async_computation.2 | async-start | bytes 524288 | tf_op jit(solution)/shard_map/all_to_all | solution.py:304
  72.3 9.0 %collective-permute-start.4 = (bf16[2,6,6,512]{3,2,1,0:T(8,128)(2,1)S(1)}, bf16[2,6,6,512]{3,2,1,0:T(8,128)(2,1)S(1)}, u32[]{:S(2)}, u32[]{:S(2)}) collective-permute-start(bf16[2,6,6,512]{3,2,1,0:T(8,128)(2,1)S(1)} %get-tuple-element.29), channel_id=1, source_target_pairs={{0,64},{64,128},{128,192},{192,256},{256,320},{320,384},{384,448},... | collective-permute-start | bytes 221192 | tf_op jit(solution)/shard_map/ppermute | solution.py:284

commit v6 on v5

--- a/solution.py
+++ b/solution.py
@@ -90,7 +90,7 @@
 
 
 def forward_kernel(
-    last_ref, tok_ref, cot_ref, lon_ref, lat_ref, diag_ref, wq_ref, wk_ref, wv_ref,
+    last_ref, tok_ref, cot_ref, diag_ref, lat_ref, lon_ref, wq_ref, wk_ref, wv_ref,
     g_ref, q_ref, k_ref, v_ref, c_ref,
     x_s, c_s, ot_s,
 ):
@@ -129,7 +129,7 @@
     c_ref[...] = c
 
 
-def forward_call(last, tokens, cotangent, lon, lat, diag, wq, wk, wv):
+def forward_call(last, tokens, cotangent, diag, lat, lon, wq, wk, wv):
     flat = jax.ShapeDtypeStruct((N, D), BF16)
     return pl.pallas_call(
         forward_kernel,
@@ -142,7 +142,7 @@
             pltpu.VMEM((D, N), BF16),
         ],
         compiler_params=PARAMS,
-    )(last, tokens, cotangent, lon, lat, diag, wq, wk, wv)
+    )(last, tokens, cotangent, diag, lat, lon, wq, wk, wv)
 
 
 def backward_kernel(
@@ -285,12 +285,12 @@
 
 
 def per_device(tokens, cotangent, w_query, w_key, w_value, w_output):
+    diag = shifted(jnp.stack([tokens[:HALF, :HALF], cotangent[:HALF, :HALF]]), -1, -1)
     lat = shifted(jnp.stack([tokens[:HALF, HALF:], cotangent[:HALF, HALF:]]), -1, 0)
     lon = shifted(jnp.stack([tokens[HALF:, :HALF], cotangent[HALF:, :HALF]]), 0, -1)
-    diag = shifted(jnp.stack([tokens[:HALF, :HALF], cotangent[:HALF, :HALF]]), -1, -1)
     last = (lax.axis_index(LAT) == lax.axis_size(LAT) - 1).astype(jnp.int32).reshape(1)
     wq, wk, wv, wo = load_weights(w_query, w_key, w_value, w_output)
-    g, q, k, v, c = forward_call(last, tokens, cotangent, lon, lat, diag, wq, wk, wv)
+    g, q, k, v, c = forward_call(last, tokens, cotangent, diag, lat, lon, wq, wk, wv)
     n_chips = lax.axis_size(CHIPS)
     n_far = lax.axis_size("zh")
     parts = g.reshape(2 * n_chips, ROWS, COLS)

time: 83.4 us -> 81.2 us (0.974)
  starting transfers between devices: 43.6 us -> 41.4 us
    all_to_all x1, starting transfers between devices: 7.5 us -> 6.34 us  [per_device(): parts = lax.all_to_all(parts, BLOCK, 0, 0, tiled=True)]
    ppermute x5, starting transfers between devices: 28.4 us -> 27.3 us  [shifted(): return lax.ppermute(value, axes, pairs)]
where the time goes in v6:
time: 81.2 us; the launch traced here: 80.5 us
  starting transfers between devices  41.4 us (51%)
  blocking collectives  18.6 us (23%)
  Pallas kernels  9.64 us (12%)
  waiting for transfers between devices  8.88 us (11%)
  local copies, waits for them, and re-layouts  1.07 us (1%)
    ppermute x5, starting transfers between devices, shifted(): return lax.ppermute(value, axes, pairs)  27.3 us
    all_to_all x1, blocking collectives, per_device(): lax.all_to_all(parts, 'zh', 0, 0, axis_index_groups=[FAR_ORDER], tiled=True)  14.4 us
    all_to_all x1, starting transfers between devices, per_device(): lax.all_to_all(parts, CHIPS, 0, 0, axis_index_groups=[CHIP_ORDER], tiled=...  7.71 us
    all_to_all x1, starting transfers between devices, per_device(): parts = lax.all_to_all(parts, BLOCK, 0, 0, tiled=True)  6.34 us
    all_to_all x1, waiting for transfers between devices, per_device(): parts = lax.all_to_all(parts, BLOCK, 0, 0, tiled=True)  4.67 us
    all_gather x1, blocking collectives, per_device(): parts = lax.all_gather(parts, 'core', axis=1, tiled=True)  4.25 us
    ppermute x5, waiting for transfers between devices, shifted(): return lax.ppermute(value, axes, pairs)  3.47 us
    pallas_call x1, Pallas kernels, backward_call(): pl.pallas_call(backward_kernel, out_shape=(quad, quad, jax.ShapeDtypeStru...  2.7 us
  transfers between devices with their start and end apart: 7, of which 4 were waited for; matrix products, arithmetic and copies ran while one was open for 0% of the time, Pallas kernels for 6%

profile of v6, /device:TPU:1, one launch (start us, length us, event | category | flops | bytes accessed | tf_op | source)
XLA Modules:
  0.0 80.5 jit_solution(3436462150140917364)
XLA Ops:
  0.6 1.1 %slice_bitcast_fusion = (bf16[1,6,6,512]{3,2,1,0:T(8,128)(2,1)S(1)}, bf16[1,6,6,512]{3,2,1,0:T(8,128)(2,1)S(1)}, bf16[1,6,6,512]{3,2,1,0:T(8,128)(2,1)S(1)}, bf1...) fusion(bf16[12,12,512]{2,1,0:T(8,128)(2,1)} %cot_ref.1, ...), kind=kLoop, calls=%fused_computation.3 | loop fusion | bytes 442368 | tf_op jit(solution)/shard_map/stack | solution.py:290
  1.7 8.5 %collective-permute-start = (bf16[2,6,6,512]{3,2,1,0:T(8,128)(2,1)S(1)}, bf16[2,6,6,512]{3,2,1,0:T(8,128)(2,1)S(1)}, u32[]{:S(2)}, u32[]{:S(2)}) collective-permute-start(bf16[2,6,6,512]{3,2,1,0:T(8,128)(2,1)S(1)} %pad_maximum_fusion), channel_id=1, source_target_pairs={{0,511},{1,448},{2,449},{3,450},{4,451},{5,452},{6,453},{7,454},{8... | collective-permute-start | bytes 221192 | tf_op jit(solution)/shard_map/ppermute | solution.py:284
  10.3 2.1 %collective-permute-start.1 = (bf16[2,6,6,512]{3,2,1,0:T(8,128)(2,1)S(1)}, bf16[2,6,6,512]{3,2,1,0:T(8,128)(2,1)S(1)}, u32[]{:S(2)}, u32[]{:S(2)}) collective-permute-start(bf16[2,6,6,512]{3,2,1,0:T(8,128)(2,1)S(1)} %pad_maximum_fusion.1), channel_id=1, source_target_pairs={{0,448},{64,0},{128,64},{192,128},{256,192},{320,256},{384,320},{4... | collective-permute-start | bytes 221192 | tf_op jit(solution)/shard_map/ppermute | solution.py:284
  12.4 11.0 %collective-permute-start.2 = (bf16[2,6,6,512]{3,2,1,0:T(8,128)(2,1)S(1)}, bf16[2,6,6,512]{3,2,1,0:T(8,128)(2,1)S(1)}, u32[]{:S(2)}, u32[]{:S(2)}) collective-permute-start(bf16[2,6,6,512]{3,2,1,0:T(8,128)(2,1)S(1)} %pad_maximum_fusion.2), channel_id=1, source_target_pairs={{0,63},{1,0},{2,1},{3,2},{4,3},{5,4},{6,5},{7,6},{8,7},{9,8},{10,9... | collective-permute-start | bytes 221192 | tf_op jit(solution)/shard_map/ppermute | solution.py:284
  23.4 0.0 copy-start
  23.4 0.0 copy-start.1
  23.4 2.4 %shard_map.77 = (bf16[512,512]{1,0:T(8,128)(2,1)S(1)}, bf16[512,512]{1,0:T(8,128)(2,1)S(1)}, bf16[512,512]{1,0:T(8,128)(2,1)S(1)}, bf16[512,512]{1,0:T(8,128)(2,1)}) custom-call(bf16[512,512]{1,0:T(8,128)(2,1)} %wq_ref.1, bf16[512,512]{1,0:T(8,128)(2,1)} %wk_ref.1, bf16[512,512]{1,0:T(8,128)(2,1)} %wv_ref.1, bf16[512,512]{1,0:T(8,128)(2,1)} %wo_ref.1), custom_call_target="tpu_custom_call" | custom-call | tf_op jit(solution)/shard_map/pallas_call | solution.py:57
  25.8 0.0 collective-permute-done.diag_ref
  25.9 0.0 collective-permute-done.1.lat_ref
  25.9 0.0 collective-permute-done.2.lon_ref
  25.9 0.0 copy-done
  25.9 0.0 copy-done.1
  25.9 2.4 %shard_map.78 = (bf16[2,32,16,256]{3,2,1,0:T(8,128)(2,1)}, bf16[144,512]{1,0:T(8,128)(2,1)S(1)}, bf16[144,512]{1,0:T(8,128)(2,1)S(1)}, bf16[144,512]{1,0:T(8,128)(2,1)S(1)}, bf16[144,512]{1,0:T(8,128)(2,1)S(1)}) custom-call(s32[1]{0:T(128)} %bitcast.last_ref, bf16[12,12,512]{2,1,0:T(8,128)(2,1)S(1)} %copy-done, bf16[12,12,512]{2,1,0:T(8,128)(2,1)S(1)} %copy-done.1, ...), custom_call_target="tpu_custom_call" | custom-call | tf_op jit(solution)/shard_map/pallas_call | solution.py:134
  28.3 0.0 copy-start.2
  28.3 6.3 %all-to-all-start = ((bf16[64,16,256]{2,1,0:T(8,128)(2,1)}), bf16[64,16,256]{2,1,0:T(8,128)(2,1)S(1)}, u32[]{:S(2)}, u32[]{:S(2)}) async-start(bf16[64,16,256]{2,1,0:T(8,128)(2,1)} %bitcast.7), calls=%async_computation | async-start | bytes 1048576 | tf_op jit(solution)/shard_map/all_to_all | solution.py:297
  34.7 0.0 copy-done.2
  34.7 2.7 %shard_map.79 = (bf16[6,6,512]{2,1,0:T(8,128)(2,1)S(1)}, bf16[6,6,512]{2,1,0:T(8,128)(2,1)S(1)}, bf16[2,6,6,512]{3,2,1,0:T(8,128)(2,1)S(1)}) custom-call(s32[1]{0:T(128)} %bitcast.last_ref, bf16[144,512]{1,0:T(8,128)(2,1)S(1)} %get-tuple-element.20.q_ref, bf16[144,512]{1,0:T(8,128)(2,1)S(1)} %get-tuple-element.21.k_ref, ...), custom_call_target="tpu_custom_call" | custom-call | tf_op jit(solution)/shard_map/pallas_call | solution.py:189
  37.4 3.5 %collective-permute-start.3 = (bf16[2,6,6,512]{3,2,1,0:T(8,128)(2,1)S(1)}, bf16[2,6,6,512]{3,2,1,0:T(8,128)(2,1)S(1)}, u32[]{:S(2)}, u32[]{:S(2)}) collective-permute-start(bf16[2,6,6,512]{3,2,1,0:T(8,128)(2,1)S(1)} %get-tuple-element.26), channel_id=1, source_target_pairs={{0,1},{1,2},{2,3},{3,4},{4,5},{5,6},{6,7},{7,8},{8,9},{9,10},{10,1... | collective-permute-start | bytes 221192 | tf_op jit(solution)/shard_map/ppermute | solution.py:284
  40.9 1.7 %collective-permute-done.3.side_ref = bf16[2,6,6,512]{3,2,1,0:T(8,128)(2,1)S(1)} collective-permute-done((bf16[2,6,6,512]{3,2,1,0:T(8,128)(2,1)S(1)}, bf16[2,6,6,512]{3,2,1,0:T(8,128)(2,1)S(1)}, u32[]{:S(2)}, u32[]{:S(2)}) %collective-permute-start.3) | collective-permute-done | bytes 73760 | tf_op jit(solution)/shard_map/ppermute | solution.py:284
  42.6 4.7 %all-to-all-done.in_ref = bf16[64,16,256]{2,1,0:T(8,128)(2,1)S(1)} async-done(((bf16[64,16,256]{2,1,0:T(8,128)(2,1)}), bf16[64,16,256]{2,1,0:T(8,128)(2,1)S(1)}, u32[]{:S(2)}, u32[]{:S(2)}) %all-to-all-start) | async-done | bytes 524320 | tf_op jit(solution)/shard_map/all_to_all | solution.py:297
  47.3 0.1 shard_map.80
  47.4 14.4 %all_to_all.15.in_ref = bf16[8,16,256]{2,1,0:T(8,128)(2,1)S(1)} all-to-all(bf16[8,16,256]{2,1,0:T(8,128)(2,1)S(1)} %get-tuple-element.27), channel_id=1, replica_groups={{32,40,48,56,0,8,16,24},{33,41,49,57,1,9,17,25},{34,42,50,58,2,10,18,26..., dimensions={0} | all-to-all | bytes 131072 | tf_op jit(solution)/shard_map/all_to_all | solution.py:301
  61.7 0.7 shard_map.81
  62.5 7.7 %all-to-all-start.2 = ((bf16[32,16,256]{2,1,0:T(8,128)(2,1)}), bf16[32,16,256]{2,1,0:T(8,128)(2,1)S(1)}, u32[]{:S(2)}, u32[]{:S(2)}) async-start(bf16[32,16,256]{2,1,0:T(8,128)(2,1)} %shard_map.81), calls=%async_computation.2 | async-start | bytes 524288 | tf_op jit(solution)/shard_map/all_to_all | solution.py:304
  70.2 2.2 %collective-permute-start.4 = (bf16[2,6,6,512]{3,2,1,0:T(8,128)(2,1)S(1)}, bf16[2,6,6,512]{3,2,1,0:T(8,128)(2,1)S(1)}, u32[]{:S(2)}, u32[]{:S(2)}) collective-permute-start(bf16[2,6,6,512]{3,2,1,0:T(8,128)(2,1)S(1)} %get-tuple-element.29), channel_id=1, source_target_pairs={{0,64},{64,128},{128,192},{192,256},{256,320},{320,384},{384,448},... | collective-permute-start | bytes 221192 | tf_op jit(solution)/shard_map/ppermute | solution.py:284
  72.4 0.7 all-to-all-done.2
  73.1 4.3 %all-gather = bf16[32,32,256]{2,1,0:T(8,128)(2,1)S(1)} all-gather(bf16[32,16,256]{2,1,0:T(8,128)(2,1)S(1)} %all-to-all-done.2), channel_id=2, replica_groups=mesh['y'=4,'xh'=2,'zh'=8,'zl'=2,'xl'=2,'core'=2] {'core'}, dimensions={1}, use_global_device_ids=true | all-gather | bytes 786432 | tf_op jit(solution)/shard_map/all_gather | solution.py:306
  77.4 1.8 %collective-permute-done.4.above_ref = bf16[2,6,6,512]{3,2,1,0:T(8,128)(2,1)S(1)} collective-permute-done((bf16[2,6,6,512]{3,2,1,0:T(8,128)(2,1)S(1)}, bf16[2,6,6,512]{3,2,1,0:T(8,128)(2,1)S(1)}, u32[]{:S(2)}, u32[]{:S(2)}) %collective-permute-start.4) | collective-permute-done | bytes 73760 | tf_op jit(solution)/shard_map/ppermute | solution.py:284
  79.2 1.3 %shard_map.82 = (bf16[12,12,512]{2,1,0:T(8,128)(2,1)}, f32[512,512]{1,0:T(8,128)}) custom-call(bf16[64,16,256]{2,1,0:T(8,128)(2,1)S(1)} %bitcast.15, bf16[6,6,512]{2,1,0:T(8,128)(2,1)S(1)} %get-tuple-element.28.own_ref, bf16[2,6,6,512]{3,2,1,0:T(8,128)(2,1)S(1)} %collective-permute-done.3.side_ref, bf16[2,6,6,512]{3,2,1,0:T(8,128)(2,1)S(1)} %collective-permute-done.4.above_ref), custom_call_target="tpu_custom_call" | custom-call | tf_op jit(solution)/shard_map/pallas_call | solution.py:263
  (3 shorter events, 0.1 us)
Async XLA Ops:
  1.7 24.1 %collective-permute-start = (bf16[2,6,6,512]{3,2,1,0:T(8,128)(2,1)S(1)}, bf16[2,6,6,512]{3,2,1,0:T(8,128)(2,1)S(1)}, u32[]{:S(2)}, u32[]{:S(2)}) collective-permute-start(bf16[2,6,6,512]{3,2,1,0:T(8,128)(2,1)S(1)} %pad_maximum_fusion), channel_id=1, source_target_pairs={{0,511},{1,448},{2,449},{3,450},{4,451},{5,452},{6,453},{7,454},{8... | collective-permute-start | bytes 221192 | tf_op jit(solution)/shard_map/ppermute | solution.py:284
  10.3 15.6 %collective-permute-start.1 = (bf16[2,6,6,512]{3,2,1,0:T(8,128)(2,1)S(1)}, bf16[2,6,6,512]{3,2,1,0:T(8,128)(2,1)S(1)}, u32[]{:S(2)}, u32[]{:S(2)}) collective-permute-start(bf16[2,6,6,512]{3,2,1,0:T(8,128)(2,1)S(1)} %pad_maximum_fusion.1), channel_id=1, source_target_pairs={{0,448},{64,0},{128,64},{192,128},{256,192},{320,256},{384,320},{4... | collective-permute-start | bytes 221192 | tf_op jit(solution)/shard_map/ppermute | solution.py:284
  12.4 13.4 %collective-permute-start.2 = (bf16[2,6,6,512]{3,2,1,0:T(8,128)(2,1)S(1)}, bf16[2,6,6,512]{3,2,1,0:T(8,128)(2,1)S(1)}, u32[]{:S(2)}, u32[]{:S(2)}) collective-permute-start(bf16[2,6,6,512]{3,2,1,0:T(8,128)(2,1)S(1)} %pad_maximum_fusion.2), channel_id=1, source_target_pairs={{0,63},{1,0},{2,1},{3,2},{4,3},{5,4},{6,5},{7,6},{8,7},{9,8},{10,9... | collective-permute-start | bytes 221192 | tf_op jit(solution)/shard_map/ppermute | solution.py:284
  23.4 2.5 %copy-start = (bf16[12,12,512]{2,1,0:T(8,128)(2,1)S(1)}, bf16[12,12,512]{2,1,0:T(8,128)(2,1)}, u32[]{:S(2)}) copy-start(bf16[12,12,512]{2,1,0:T(8,128)(2,1)} %tok_ref.1) | copy-start | bytes 442372
  23.4 2.5 %copy-start.1 = (bf16[12,12,512]{2,1,0:T(8,128)(2,1)S(1)}, bf16[12,12,512]{2,1,0:T(8,128)(2,1)}, u32[]{:S(2)}) copy-start(bf16[12,12,512]{2,1,0:T(8,128)(2,1)} %cot_ref.1) | copy-start | bytes 442372
  28.3 6.3 %copy-start.2 = (bf16[512,512]{1,0:T(8,128)(2,1)S(1)}, bf16[512,512]{1,0:T(8,128)(2,1)}, u32[]{:S(2)}) copy-start(bf16[512,512]{1,0:T(8,128)(2,1)} %get-tuple-element.24.wo_ref) | copy-start | bytes 1572868
  28.3 19.0 %all-to-all-start = ((bf16[64,16,256]{2,1,0:T(8,128)(2,1)}), bf16[64,16,256]{2,1,0:T(8,128)(2,1)S(1)}, u32[]{:S(2)}, u32[]{:S(2)}) async-start(bf16[64,16,256]{2,1,0:T(8,128)(2,1)} %bitcast.7), calls=%async_computation | async-start | bytes 1048576 | tf_op jit(solution)/shard_map/all_to_all | solution.py:297
  37.4 5.2 %collective-permute-start.3 = (bf16[2,6,6,512]{3,2,1,0:T(8,128)(2,1)S(1)}, bf16[2,6,6,512]{3,2,1,0:T(8,128)(2,1)S(1)}, u32[]{:S(2)}, u32[]{:S(2)}) collective-permute-start(bf16[2,6,6,512]{3,2,1,0:T(8,128)(2,1)S(1)} %get-tuple-element.26), channel_id=1, source_target_pairs={{0,1},{1,2},{2,3},{3,4},{4,5},{5,6},{6,7},{7,8},{8,9},{9,10},{10,1... | collective-permute-start | bytes 221192 | tf_op jit(solution)/shard_map/ppermute | solution.py:284
  62.5 10.7 %all-to-all-start.2 = ((bf16[32,16,256]{2,1,0:T(8,128)(2,1)}), bf16[32,16,256]{2,1,0:T(8,128)(2,1)S(1)}, u32[]{:S(2)}, u32[]{:S(2)}) async-start(bf16[32,16,256]{2,1,0:T(8,128)(2,1)} %shard_map.81), calls=%async_computation.2 | async-start | bytes 524288 | tf_op jit(solution)/shard_map/all_to_all | solution.py:304
  70.2 9.0 %collective-permute-start.4 = (bf16[2,6,6,512]{3,2,1,0:T(8,128)(2,1)S(1)}, bf16[2,6,6,512]{3,2,1,0:T(8,128)(2,1)S(1)}, u32[]{:S(2)}, u32[]{:S(2)}) collective-permute-start(bf16[2,6,6,512]{3,2,1,0:T(8,128)(2,1)S(1)} %get-tuple-element.29), channel_id=1, source_target_pairs={{0,64},{64,128},{128,192},{192,256},{256,320},{320,384},{384,448},... | collective-permute-start | bytes 221192 | tf_op jit(solution)/shard_map/ppermute | solution.py:284

commit v7 on v6

--- a/solution.py
+++ b/solution.py
@@ -41,8 +41,8 @@
     return lax.dot_general(a, b, dims, preferred_element_type=F32)
 
 
-def load_kernel(wq_ref, wk_ref, wv_ref, wo_ref, q_out, k_out, v_out, o_out, sems):
-    pairs = ((wq_ref, q_out), (wk_ref, k_out), (wv_ref, v_out), (wo_ref, o_out))
+def load_kernel(wq_ref, wk_ref, wv_ref, q_out, k_out, v_out, sems):
+    pairs = ((wq_ref, q_out), (wk_ref, k_out), (wv_ref, v_out))
     copies = [
         pltpu.make_async_copy(source, target, sems.at[i])
         for i, (source, target) in enumerate(pairs)
@@ -57,9 +57,9 @@
     return pl.pallas_call(
         load_kernel,
         out_shape=tuple(jax.ShapeDtypeStruct(w.shape, w.dtype) for w in weights),
-        in_specs=[HBM] * 4,
-        out_specs=(VMEM,) * 4,
-        scratch_shapes=[pltpu.SemaphoreType.DMA((4,))],
+        in_specs=[HBM] * 3,
+        out_specs=(VMEM,) * 3,
+        scratch_shapes=[pltpu.SemaphoreType.DMA((3,))],
         compiler_params=WIDE,
     )(*weights)
 
@@ -289,13 +289,13 @@
     lat = shifted(jnp.stack([tokens[:HALF, HALF:], cotangent[:HALF, HALF:]]), -1, 0)
     lon = shifted(jnp.stack([tokens[HALF:, :HALF], cotangent[HALF:, :HALF]]), 0, -1)
     last = (lax.axis_index(LAT) == lax.axis_size(LAT) - 1).astype(jnp.int32).reshape(1)
-    wq, wk, wv, wo = load_weights(w_query, w_key, w_value, w_output)
+    wq, wk, wv = load_weights(w_query, w_key, w_value)
     g, q, k, v, c = forward_call(last, tokens, cotangent, diag, lat, lon, wq, wk, wv)
     n_chips = lax.axis_size(CHIPS)
     n_far = lax.axis_size("zh")
     parts = g.reshape(2 * n_chips, ROWS, COLS)
     parts = lax.all_to_all(parts, BLOCK, 0, 0, tiled=True)
-    own, lat, side = backward_call(last, q, k, v, c, wq, wk, wv, wo)
+    own, lat, side = backward_call(last, q, k, v, c, wq, wk, wv, w_output)
     side = shifted(side, 0, 1)
     parts, above = sum_and_join(parts, n_far, lat, side)
     parts = lax.all_to_all(parts, "zh", 0, 0, axis_index_groups=[FAR_ORDER], tiled=True)

time: 81.2 us -> 81.2 us (level)
  Pallas kernels: 9.64 us -> 8.67 us
    pallas_call x1, Pallas kernels: 2.39 us -> 1.44 us  [load_weights(): pl.pallas_call(load_kernel, out_shape=tuple((jax.ShapeDtypeStruct(w.shape...]
  transfers between devices with their start and end apart: 7 -> 7, of which waited for: 4 -> 4; matrix products, arithmetic and copies ran while one was open for 0% -> 0% of each run, Pallas kernels for 6% -> 5%
where the time goes in v7:
time: 81.2 us; the launch traced here: 80.5 us
  starting transfers between devices  42 us (52%)
  blocking collectives  18.9 us (23%)
  waiting for transfers between devices  8.88 us (11%)
  Pallas kernels  8.67 us (11%)
  local copies, waits for them, and re-layouts  1.07 us (1%)
    ppermute x5, starting transfers between devices, shifted(): return lax.ppermute(value, axes, pairs)  27.3 us
    all_to_all x1, blocking collectives, per_device(): lax.all_to_all(parts, 'zh', 0, 0, axis_index_groups=[FAR_ORDER], tiled=True)  14.7 us
    all_to_all x1, starting transfers between devices, per_device(): lax.all_to_all(parts, CHIPS, 0, 0, axis_index_groups=[CHIP_ORDER], tiled=...  7.7 us
    all_to_all x1, starting transfers between devices, per_device(): parts = lax.all_to_all(parts, BLOCK, 0, 0, tiled=True)  7 us
    all_to_all x1, waiting for transfers between devices, per_device(): parts = lax.all_to_all(parts, BLOCK, 0, 0, tiled=True)  4.67 us
    all_gather x1, blocking collectives, per_device(): parts = lax.all_gather(parts, 'core', axis=1, tiled=True)  4.25 us
    ppermute x5, waiting for transfers between devices, shifted(): return lax.ppermute(value, axes, pairs)  3.47 us
    pallas_call x1, Pallas kernels, backward_call(): pl.pallas_call(backward_kernel, out_shape=(quad, quad, jax.ShapeDtypeStru...  2.7 us
  transfers between devices with their start and end apart: 7, of which 4 were waited for; matrix products, arithmetic and copies ran while one was open for 0% of the time, Pallas kernels for 5%

profile of v7, /device:TPU:1, one launch (start us, length us, event | category | flops | bytes accessed | tf_op | source)
XLA Modules:
  0.0 80.5 jit_solution(9893441340800973928)
XLA Ops:
  0.6 1.1 %slice_bitcast_fusion = (bf16[1,6,6,512]{3,2,1,0:T(8,128)(2,1)S(1)}, bf16[1,6,6,512]{3,2,1,0:T(8,128)(2,1)S(1)}, bf16[1,6,6,512]{3,2,1,0:T(8,128)(2,1)S(1)}, bf1...) fusion(bf16[12,12,512]{2,1,0:T(8,128)(2,1)} %cot_ref.1, ...), kind=kLoop, calls=%fused_computation.3 | loop fusion | bytes 442368 | tf_op jit(solution)/shard_map/stack | solution.py:290
  1.7 8.5 %collective-permute-start = (bf16[2,6,6,512]{3,2,1,0:T(8,128)(2,1)S(1)}, bf16[2,6,6,512]{3,2,1,0:T(8,128)(2,1)S(1)}, u32[]{:S(2)}, u32[]{:S(2)}) collective-permute-start(bf16[2,6,6,512]{3,2,1,0:T(8,128)(2,1)S(1)} %pad_maximum_fusion), channel_id=1, source_target_pairs={{0,511},{1,448},{2,449},{3,450},{4,451},{5,452},{6,453},{7,454},{8... | collective-permute-start | bytes 221192 | tf_op jit(solution)/shard_map/ppermute | solution.py:284
  10.3 2.1 %collective-permute-start.1 = (bf16[2,6,6,512]{3,2,1,0:T(8,128)(2,1)S(1)}, bf16[2,6,6,512]{3,2,1,0:T(8,128)(2,1)S(1)}, u32[]{:S(2)}, u32[]{:S(2)}) collective-permute-start(bf16[2,6,6,512]{3,2,1,0:T(8,128)(2,1)S(1)} %pad_maximum_fusion.1), channel_id=1, source_target_pairs={{0,448},{64,0},{128,64},{192,128},{256,192},{320,256},{384,320},{4... | collective-permute-start | bytes 221192 | tf_op jit(solution)/shard_map/ppermute | solution.py:284
  12.4 11.0 %collective-permute-start.2 = (bf16[2,6,6,512]{3,2,1,0:T(8,128)(2,1)S(1)}, bf16[2,6,6,512]{3,2,1,0:T(8,128)(2,1)S(1)}, u32[]{:S(2)}, u32[]{:S(2)}) collective-permute-start(bf16[2,6,6,512]{3,2,1,0:T(8,128)(2,1)S(1)} %pad_maximum_fusion.2), channel_id=1, source_target_pairs={{0,63},{1,0},{2,1},{3,2},{4,3},{5,4},{6,5},{7,6},{8,7},{9,8},{10,9... | collective-permute-start | bytes 221192 | tf_op jit(solution)/shard_map/ppermute | solution.py:284
  23.4 0.0 copy-start
  23.4 0.0 copy-start.1
  23.4 1.4 %shard_map.77 = (bf16[512,512]{1,0:T(8,128)(2,1)S(1)}, bf16[512,512]{1,0:T(8,128)(2,1)S(1)}, bf16[512,512]{1,0:T(8,128)(2,1)S(1)}) custom-call(bf16[512,512]{1,0:T(8,128)(2,1)} %wq_ref.1, bf16[512,512]{1,0:T(8,128)(2,1)} %wk_ref.1, bf16[512,512]{1,0:T(8,128)(2,1)} %wv_ref.1), custom_call_target="tpu_custom_call" | custom-call | tf_op jit(solution)/shard_map/pallas_call | solution.py:57
  24.9 0.0 collective-permute-done.diag_ref
  24.9 0.0 collective-permute-done.1.lat_ref
  24.9 0.0 collective-permute-done.2.lon_ref
  24.9 0.0 copy-done
  24.9 0.0 copy-done.1
  24.9 2.4 %shard_map.78 = (bf16[2,32,16,256]{3,2,1,0:T(8,128)(2,1)}, bf16[144,512]{1,0:T(8,128)(2,1)S(1)}, bf16[144,512]{1,0:T(8,128)(2,1)S(1)}, bf16[144,512]{1,0:T(8,128)(2,1)S(1)}, bf16[144,512]{1,0:T(8,128)(2,1)S(1)}) custom-call(s32[1]{0:T(128)} %bitcast.last_ref, bf16[12,12,512]{2,1,0:T(8,128)(2,1)S(1)} %copy-done, bf16[12,12,512]{2,1,0:T(8,128)(2,1)S(1)} %copy-done.1, ...), custom_call_target="tpu_custom_call" | custom-call | tf_op jit(solution)/shard_map/pallas_call | solution.py:134
  27.3 0.0 copy-start.2
  27.3 7.0 %all-to-all-start = ((bf16[64,16,256]{2,1,0:T(8,128)(2,1)}), bf16[64,16,256]{2,1,0:T(8,128)(2,1)S(1)}, u32[]{:S(2)}, u32[]{:S(2)}) async-start(bf16[64,16,256]{2,1,0:T(8,128)(2,1)} %bitcast.7), calls=%async_computation | async-start | bytes 1048576 | tf_op jit(solution)/shard_map/all_to_all | solution.py:297
  34.4 0.0 copy-done.2
  34.4 2.7 %shard_map.79 = (bf16[6,6,512]{2,1,0:T(8,128)(2,1)S(1)}, bf16[6,6,512]{2,1,0:T(8,128)(2,1)S(1)}, bf16[2,6,6,512]{3,2,1,0:T(8,128)(2,1)S(1)}) custom-call(s32[1]{0:T(128)} %bitcast.last_ref, bf16[144,512]{1,0:T(8,128)(2,1)S(1)} %get-tuple-element.19.q_ref, bf16[144,512]{1,0:T(8,128)(2,1)S(1)} %get-tuple-element.20.k_ref, ...), custom_call_target="tpu_custom_call" | custom-call | tf_op jit(solution)/shard_map/pallas_call | solution.py:189
  37.1 3.5 %collective-permute-start.3 = (bf16[2,6,6,512]{3,2,1,0:T(8,128)(2,1)S(1)}, bf16[2,6,6,512]{3,2,1,0:T(8,128)(2,1)S(1)}, u32[]{:S(2)}, u32[]{:S(2)}) collective-permute-start(bf16[2,6,6,512]{3,2,1,0:T(8,128)(2,1)S(1)} %get-tuple-element.24), channel_id=1, source_target_pairs={{0,1},{1,2},{2,3},{3,4},{4,5},{5,6},{6,7},{7,8},{8,9},{9,10},{10,1... | collective-permute-start | bytes 221192 | tf_op jit(solution)/shard_map/ppermute | solution.py:284
  40.6 1.7 %collective-permute-done.3.side_ref = bf16[2,6,6,512]{3,2,1,0:T(8,128)(2,1)S(1)} collective-permute-done((bf16[2,6,6,512]{3,2,1,0:T(8,128)(2,1)S(1)}, bf16[2,6,6,512]{3,2,1,0:T(8,128)(2,1)S(1)}, u32[]{:S(2)}, u32[]{:S(2)}) %collective-permute-start.3) | collective-permute-done | bytes 73760 | tf_op jit(solution)/shard_map/ppermute | solution.py:284
  42.3 4.7 %all-to-all-done.in_ref = bf16[64,16,256]{2,1,0:T(8,128)(2,1)S(1)} async-done(((bf16[64,16,256]{2,1,0:T(8,128)(2,1)}), bf16[64,16,256]{2,1,0:T(8,128)(2,1)S(1)}, u32[]{:S(2)}, u32[]{:S(2)}) %all-to-all-start) | async-done | bytes 524320 | tf_op jit(solution)/shard_map/all_to_all | solution.py:297
  47.0 0.1 shard_map.80
  47.1 14.7 %all_to_all.15.in_ref = bf16[8,16,256]{2,1,0:T(8,128)(2,1)S(1)} all-to-all(bf16[8,16,256]{2,1,0:T(8,128)(2,1)S(1)} %get-tuple-element.25), channel_id=1, replica_groups={{32,40,48,56,0,8,16,24},{33,41,49,57,1,9,17,25},{34,42,50,58,2,10,18,26..., dimensions={0} | all-to-all | bytes 131072 | tf_op jit(solution)/shard_map/all_to_all | solution.py:301
  61.7 0.7 shard_map.81
  62.5 7.7 %all-to-all-start.2 = ((bf16[32,16,256]{2,1,0:T(8,128)(2,1)}), bf16[32,16,256]{2,1,0:T(8,128)(2,1)S(1)}, u32[]{:S(2)}, u32[]{:S(2)}) async-start(bf16[32,16,256]{2,1,0:T(8,128)(2,1)} %shard_map.81), calls=%async_computation.2 | async-start | bytes 524288 | tf_op jit(solution)/shard_map/all_to_all | solution.py:304
  70.2 2.2 %collective-permute-start.4 = (bf16[2,6,6,512]{3,2,1,0:T(8,128)(2,1)S(1)}, bf16[2,6,6,512]{3,2,1,0:T(8,128)(2,1)S(1)}, u32[]{:S(2)}, u32[]{:S(2)}) collective-permute-start(bf16[2,6,6,512]{3,2,1,0:T(8,128)(2,1)S(1)} %get-tuple-element.27), channel_id=1, source_target_pairs={{0,64},{64,128},{128,192},{192,256},{256,320},{320,384},{384,448},... | collective-permute-start | bytes 221192 | tf_op jit(solution)/shard_map/ppermute | solution.py:284
  72.4 0.7 all-to-all-done.2
  73.1 4.3 %all-gather = bf16[32,32,256]{2,1,0:T(8,128)(2,1)S(1)} all-gather(bf16[32,16,256]{2,1,0:T(8,128)(2,1)S(1)} %all-to-all-done.2), channel_id=2, replica_groups=mesh['y'=4,'xh'=2,'zh'=8,'zl'=2,'xl'=2,'core'=2] {'core'}, dimensions={1}, use_global_device_ids=true | all-gather | bytes 786432 | tf_op jit(solution)/shard_map/all_gather | solution.py:306
  77.4 1.8 %collective-permute-done.4.above_ref = bf16[2,6,6,512]{3,2,1,0:T(8,128)(2,1)S(1)} collective-permute-done((bf16[2,6,6,512]{3,2,1,0:T(8,128)(2,1)S(1)}, bf16[2,6,6,512]{3,2,1,0:T(8,128)(2,1)S(1)}, u32[]{:S(2)}, u32[]{:S(2)}) %collective-permute-start.4) | collective-permute-done | bytes 73760 | tf_op jit(solution)/shard_map/ppermute | solution.py:284
  79.1 1.3 %shard_map.82 = (bf16[12,12,512]{2,1,0:T(8,128)(2,1)}, f32[512,512]{1,0:T(8,128)}) custom-call(bf16[64,16,256]{2,1,0:T(8,128)(2,1)S(1)} %bitcast.15, bf16[6,6,512]{2,1,0:T(8,128)(2,1)S(1)} %get-tuple-element.26.own_ref, bf16[2,6,6,512]{3,2,1,0:T(8,128)(2,1)S(1)} %collective-permute-done.3.side_ref, bf16[2,6,6,512]{3,2,1,0:T(8,128)(2,1)S(1)} %collective-permute-done.4.above_ref), custom_call_target="tpu_custom_call" | custom-call | tf_op jit(solution)/shard_map/pallas_call | solution.py:263
  (3 shorter events, 0.1 us)
Async XLA Ops:
  1.7 23.2 %collective-permute-start = (bf16[2,6,6,512]{3,2,1,0:T(8,128)(2,1)S(1)}, bf16[2,6,6,512]{3,2,1,0:T(8,128)(2,1)S(1)}, u32[]{:S(2)}, u32[]{:S(2)}) collective-permute-start(bf16[2,6,6,512]{3,2,1,0:T(8,128)(2,1)S(1)} %pad_maximum_fusion), channel_id=1, source_target_pairs={{0,511},{1,448},{2,449},{3,450},{4,451},{5,452},{6,453},{7,454},{8... | collective-permute-start | bytes 221192 | tf_op jit(solution)/shard_map/ppermute | solution.py:284
  10.3 14.7 %collective-permute-start.1 = (bf16[2,6,6,512]{3,2,1,0:T(8,128)(2,1)S(1)}, bf16[2,6,6,512]{3,2,1,0:T(8,128)(2,1)S(1)}, u32[]{:S(2)}, u32[]{:S(2)}) collective-permute-start(bf16[2,6,6,512]{3,2,1,0:T(8,128)(2,1)S(1)} %pad_maximum_fusion.1), channel_id=1, source_target_pairs={{0,448},{64,0},{128,64},{192,128},{256,192},{320,256},{384,320},{4... | collective-permute-start | bytes 221192 | tf_op jit(solution)/shard_map/ppermute | solution.py:284
  12.4 12.5 %collective-permute-start.2 = (bf16[2,6,6,512]{3,2,1,0:T(8,128)(2,1)S(1)}, bf16[2,6,6,512]{3,2,1,0:T(8,128)(2,1)S(1)}, u32[]{:S(2)}, u32[]{:S(2)}) collective-permute-start(bf16[2,6,6,512]{3,2,1,0:T(8,128)(2,1)S(1)} %pad_maximum_fusion.2), channel_id=1, source_target_pairs={{0,63},{1,0},{2,1},{3,2},{4,3},{5,4},{6,5},{7,6},{8,7},{9,8},{10,9... | collective-permute-start | bytes 221192 | tf_op jit(solution)/shard_map/ppermute | solution.py:284
  23.4 1.5 %copy-start = (bf16[12,12,512]{2,1,0:T(8,128)(2,1)S(1)}, bf16[12,12,512]{2,1,0:T(8,128)(2,1)}, u32[]{:S(2)}) copy-start(bf16[12,12,512]{2,1,0:T(8,128)(2,1)} %tok_ref.1) | copy-start | bytes 442372
  23.4 1.5 %copy-start.1 = (bf16[12,12,512]{2,1,0:T(8,128)(2,1)S(1)}, bf16[12,12,512]{2,1,0:T(8,128)(2,1)}, u32[]{:S(2)}) copy-start(bf16[12,12,512]{2,1,0:T(8,128)(2,1)} %cot_ref.1) | copy-start | bytes 442372
  27.3 7.0 %copy-start.2 = (bf16[512,512]{1,0:T(8,128)(2,1)S(1)}, bf16[512,512]{1,0:T(8,128)(2,1)}, u32[]{:S(2)}) copy-start(bf16[512,512]{1,0:T(8,128)(2,1)} %wo_ref.1) | copy-start | bytes 1572868
  27.3 19.6 %all-to-all-start = ((bf16[64,16,256]{2,1,0:T(8,128)(2,1)}), bf16[64,16,256]{2,1,0:T(8,128)(2,1)S(1)}, u32[]{:S(2)}, u32[]{:S(2)}) async-start(bf16[64,16,256]{2,1,0:T(8,128)(2,1)} %bitcast.7), calls=%async_computation | async-start | bytes 1048576 | tf_op jit(solution)/shard_map/all_to_all | solution.py:297
  37.1 5.2 %collective-permute-start.3 = (bf16[2,6,6,512]{3,2,1,0:T(8,128)(2,1)S(1)}, bf16[2,6,6,512]{3,2,1,0:T(8,128)(2,1)S(1)}, u32[]{:S(2)}, u32[]{:S(2)}) collective-permute-start(bf16[2,6,6,512]{3,2,1,0:T(8,128)(2,1)S(1)} %get-tuple-element.24), channel_id=1, source_target_pairs={{0,1},{1,2},{2,3},{3,4},{4,5},{5,6},{6,7},{7,8},{8,9},{9,10},{10,1... | collective-permute-start | bytes 221192 | tf_op jit(solution)/shard_map/ppermute | solution.py:284
  62.5 10.7 %all-to-all-start.2 = ((bf16[32,16,256]{2,1,0:T(8,128)(2,1)}), bf16[32,16,256]{2,1,0:T(8,128)(2,1)S(1)}, u32[]{:S(2)}, u32[]{:S(2)}) async-start(bf16[32,16,256]{2,1,0:T(8,128)(2,1)} %shard_map.81), calls=%async_computation.2 | async-start | bytes 524288 | tf_op jit(solution)/shard_map/all_to_all | solution.py:304
  70.2 9.0 %collective-permute-start.4 = (bf16[2,6,6,512]{3,2,1,0:T(8,128)(2,1)S(1)}, bf16[2,6,6,512]{3,2,1,0:T(8,128)(2,1)S(1)}, u32[]{:S(2)}, u32[]{:S(2)}) collective-permute-start(bf16[2,6,6,512]{3,2,1,0:T(8,128)(2,1)S(1)} %get-tuple-element.27), channel_id=1, source_target_pairs={{0,64},{64,128},{128,192},{192,256},{256,320},{320,384},{384,448},... | collective-permute-start | bytes 221192 | tf_op jit(solution)/shard_map/ppermute | solution.py:284
